TPU v7x, 32 devices: a whole 2x2x4 slice. The times are simulated.
32 devices in a mesh: req: 8 (over z, y), blk: 4 (over x, core).
Axes of the slice: x: 2, y: 2, z: 4, core: 2. Of those that a mesh axis runs over, the one named last changes fastest.
Arguments:
- step_inputs: bfloat16 [2, 512, 2560], P(None, 'req', 'blk'), may hold values from -6 to 6
- attention_gain: float32 [2560], replicated, may hold values from 0.25 to 1.75
- query_weight: bfloat16 [2560, 2560], P(None, 'blk'), may hold values from -0.3125 to 0.3125
- key_value_weight: bfloat16 [2560, 1024], P(None, 'blk'), may hold values from -0.125 to 0.125
- output_weight: bfloat16 [2560, 2560], P(None, 'blk'), may hold values from -0.125 to 0.125
- prompt_cache: bfloat16 [8, 48, 128, 1024], P('req', 'blk'), may hold values from -102 to 102
- page_table: int32 [8, 4, 12], P(None, 'blk'), may hold values from 0 to 11, each once within a row
- cache_lengths: int32 [8], replicated, may hold values from 1 to 6144, 24576 in all
- migration: int32 [8], replicated, may hold values from 0 to 7, each once
- parents: int32 [1, 512], P(None, 'req'), may hold values from 0 to 7
- routes: int32 [2, 512, 6], P(None, 'req'), may hold values from 0 to 63, all different within a row; in each aligned block of 64 rows (0 to 63, 64 to 127, ..., all dimensions but the last counted through in order) at most 16 rows name the same one
- feedforward_gain: float32 [2560], replicated, may hold values from 0.25 to 1.75
- router_weight: bfloat16 [2560, 64], replicated, may hold values from -0.125 to 0.125
- expert_gate: bfloat16 [64, 2560, 1536], P(('req', 'blk')), may hold values from -0.125 to 0.125
- expert_up: bfloat16 [64, 2560, 1536], P(('req', 'blk')), may hold values from -0.125 to 0.125
- expert_down: bfloat16 [64, 1536, 2560], P(('req', 'blk')), may hold values from -0.15625 to 0.15625
- shared_gate: bfloat16 [2560, 3072], P(None, 'blk'), may hold values from -0.125 to 0.125
- shared_up: bfloat16 [2560, 3072], P(None, 'blk'), may hold values from -0.125 to 0.125
- shared_down: bfloat16 [3072, 2560], P('blk'), may hold values from -0.15625 to 0.15625
Outputs:
- layer_outputs: bfloat16 [2, 512, 2560], P(None, 'req', 'blk')
Inputs may be any that keep to these rules, and one draw needn't show every extreme that they name: `routes`: in each step the 64 rows of one device along req name any one expert at most 16 times. `migration`: A permutation of the slots. Each page_table[g, c] is a permutation.
All inputs are finite; a program needn't handle non-finite values.
Results may differ from a plain program's by a relative error of at most 0.018.
The roundings to bfloat16 on the way count: a program that leaves them out, or rounds other values in their place, can miss the bound.
Values may be sent and summed in bfloat16 or wider, within the bound.
A program may use at most 128 MiB of HBM per device.

v0:
```python
import jax
import jax.numpy as jnp
from jax import lax
from jax.sharding import PartitionSpec as P

QUERY_HEADS = 20
KEY_VALUE_HEADS = 4
HEAD_WIDTH = 128
E = 64
FFE = 1536
TOPK = 6
BEAMS = 8
CAP = 16


epsilon = 1e-05
rope_base = 500000.0
masked_floor = -1e30


def joined(part, axis, combine):
    gathered = jax.tree.map(lambda a: lax.all_gather(a, axis), part)

    def take(source):
        return jax.tree.map(lambda a: lax.dynamic_index_in_dim(a, source, 0, False), gathered)

    return lax.fori_loop(
        1, lax.axis_size(axis), lambda source, state: combine(state, take(source)), take(0)
    )


def apply_rotary(vectors, position_list):
    half_width = vectors.shape[-1] // 2
    frequency = rope_base ** (-2.0 * jnp.arange(half_width, dtype=jnp.float32) / vectors.shape[-1])
    angles = position_list.astype(jnp.float32)[:, None, None] * frequency
    cosine_part = jnp.cos(angles)
    sine_part = jnp.sin(angles)
    leading = vectors[..., :half_width]
    trailing = vectors[..., half_width:]
    return jnp.concatenate(
        [
            leading * cosine_part - trailing * sine_part,
            trailing * cosine_part + leading * sine_part,
        ],
        axis=-1,
    )


def inverse_of(migration):
    slot_ids = jnp.arange(migration.shape[0], dtype=jnp.int32)
    return jnp.sum(jnp.where(migration[None, :] == slot_ids[:, None], slot_ids[None, :], 0), axis=1)


def route_pick(source_of, group_per_device, req_count):
    target = source_of.reshape(req_count, group_per_device).T
    return (target % group_per_device * req_count + target // group_per_device).reshape(-1)


def move_caches(cache_rows, source_of):
    req_count = lax.axis_size("req")
    group_per_device, span_width, features = cache_rows.shape
    pieces = cache_rows.reshape(group_per_device, req_count, span_width // req_count, features)
    spread = lax.all_to_all(pieces, "req", split_axis=1, concat_axis=1, tiled=True)
    flattened = spread.reshape(group_per_device * req_count, span_width // req_count, features)
    chosen = jnp.take(flattened, route_pick(source_of, group_per_device, req_count), axis=0)
    arrived = lax.all_to_all(
        chosen.reshape(group_per_device, req_count, span_width // req_count, features),
        "req",
        split_axis=1,
        concat_axis=1,
        tiled=True,
    )
    return arrived.reshape(group_per_device, span_width, features)


def cache_partial(query_vectors, cache_here, table_rows, lengths, blk_index, blk_count):
    group_per_device, pages_local, page_length, features = cache_here.shape
    group_of_rows = query_vectors.shape[1]
    heads_per_group = QUERY_HEADS // KEY_VALUE_HEADS
    scaling = HEAD_WIDTH ** (-0.5)
    grouped_rows = query_vectors.reshape(
        group_per_device, group_of_rows, KEY_VALUE_HEADS, heads_per_group, HEAD_WIDTH
    )
    stride = blk_count * page_length
    live = jnp.clip((lengths - blk_index * page_length + stride - 1) // stride, 0, pages_local)
    visits = jnp.max(live)
    picker = jnp.arange(group_per_device, dtype=jnp.int32)

    def visit(position_page, carried):
        score_peaks, softmax_totals, weighted_values = carried
        slot_now = lax.dynamic_index_in_dim(table_rows, position_page, 1, keepdims=False)
        loaded_pages = cache_here[picker, slot_now]
        heads_of_keys = loaded_pages[:, :, : KEY_VALUE_HEADS * HEAD_WIDTH].reshape(
            group_per_device, page_length, KEY_VALUE_HEADS, HEAD_WIDTH
        )
        heads_of_values = loaded_pages[:, :, KEY_VALUE_HEADS * HEAD_WIDTH :].reshape(
            group_per_device, page_length, KEY_VALUE_HEADS, HEAD_WIDTH
        )
        scores = (
            jnp.einsum(
                "grkqd,gtkd->grkqt", grouped_rows, heads_of_keys, preferred_element_type=jnp.float32
            )
            * scaling
        )
        position_list = (position_page * blk_count + blk_index) * page_length + jnp.arange(
            page_length, dtype=jnp.int32
        )
        valid = (position_list[None, :] < lengths[:, None])[:, None, None, None, :]
        largest = jnp.maximum(score_peaks, jnp.max(jnp.where(valid, scores, masked_floor), axis=-1))
        raised = jnp.where(valid, jnp.exp(scores - largest[..., None]), 0.0)
        factor = jnp.exp(score_peaks - largest)
        softmax_totals = softmax_totals * factor + jnp.sum(raised, axis=-1)
        weighted_values = weighted_values * factor[..., None] + jnp.einsum(
            "grkqt,gtkd->grkqd",
            raised.astype(jnp.bfloat16),
            heads_of_values,
            preferred_element_type=jnp.float32,
        )
        return (largest, softmax_totals, weighted_values)

    initial = (
        jnp.full(
            (group_per_device, group_of_rows, KEY_VALUE_HEADS, heads_per_group),
            masked_floor,
            jnp.float32,
        ),
        jnp.zeros((group_per_device, group_of_rows, KEY_VALUE_HEADS, heads_per_group), jnp.float32),
        jnp.zeros(
            (group_per_device, group_of_rows, KEY_VALUE_HEADS, heads_per_group, HEAD_WIDTH),
            jnp.float32,
        ),
    )
    score_peaks, softmax_totals, weighted_values = lax.fori_loop(0, visits, visit, initial)
    return (
        score_peaks.reshape(group_per_device, group_of_rows, QUERY_HEADS),
        softmax_totals.reshape(group_per_device, group_of_rows, QUERY_HEADS),
        weighted_values.reshape(group_per_device, group_of_rows, QUERY_HEADS, HEAD_WIDTH),
    )


def combine(earlier, later):
    largest = jnp.maximum(earlier[0], later[0])
    left_scale = jnp.exp(earlier[0] - largest)
    right_scale = jnp.exp(later[0] - largest)
    return (
        largest,
        earlier[1] * left_scale + later[1] * right_scale,
        earlier[2] * left_scale[..., None] + later[2] * right_scale[..., None],
    )


def finish_heads(
    score_peaks, softmax_totals, weighted_values, query_vectors, recent_keys, recent_values
):
    count_of_rows = query_vectors.shape[0]
    tail_length = recent_keys.shape[1]
    heads_per_group = QUERY_HEADS // KEY_VALUE_HEADS
    scaling = HEAD_WIDTH ** (-0.5)
    grouped_rows = query_vectors.reshape(
        count_of_rows, KEY_VALUE_HEADS, heads_per_group, HEAD_WIDTH
    )
    heads_of_keys = recent_keys.reshape(count_of_rows, tail_length, KEY_VALUE_HEADS, HEAD_WIDTH)
    heads_of_values = recent_values.reshape(count_of_rows, tail_length, KEY_VALUE_HEADS, HEAD_WIDTH)
    scores = (
        jnp.einsum(
            "rkqd,rtkd->rkqt", grouped_rows, heads_of_keys, preferred_element_type=jnp.float32
        )
        * scaling
    )
    score_peaks = score_peaks.reshape(count_of_rows, KEY_VALUE_HEADS, heads_per_group)
    softmax_totals = softmax_totals.reshape(count_of_rows, KEY_VALUE_HEADS, heads_per_group)
    weighted_values = weighted_values.reshape(
        count_of_rows, KEY_VALUE_HEADS, heads_per_group, HEAD_WIDTH
    )
    largest = jnp.maximum(score_peaks, jnp.max(scores, axis=-1))
    factor = jnp.exp(score_peaks - largest)
    raised = jnp.exp(scores - largest[..., None])
    softmax_totals = softmax_totals * factor + jnp.sum(raised, axis=-1)
    weighted_values = weighted_values * factor[..., None] + jnp.einsum(
        "rkqt,rtkd->rkqd",
        raised.astype(jnp.bfloat16),
        heads_of_values,
        preferred_element_type=jnp.float32,
    )
    return (
        (weighted_values / softmax_totals[..., None])
        .astype(jnp.bfloat16)
        .reshape(count_of_rows, QUERY_HEADS * HEAD_WIDTH)
    )


def per_device(
    step_inputs,
    attention_gain,
    query_weight,
    key_value_weight,
    output_weight,
    prompt_cache,
    page_table,
    cache_lengths,
    migration,
    parents,
    routes,
    feedforward_gain,
    router_weight,
    expert_gate,
    expert_up,
    expert_down,
    shared_gate,
    shared_up,
    shared_down,
):
    req_count = lax.axis_size("req")
    blk_count = lax.axis_size("blk")
    req_index = lax.axis_index("req")
    blk_index = lax.axis_index("blk")
    steps_count, rows_per_device, width_local = step_inputs.shape
    group_per_device, pages_local, page_length, features = prompt_cache.shape
    group_of_rows = rows_per_device // group_per_device
    model_width = width_local * blk_count
    slices_dev = expert_gate.shape[0]
    split_count = FFE // expert_gate.shape[2]
    inverse = inverse_of(migration)
    here = req_index * group_per_device + jnp.arange(group_per_device, dtype=jnp.int32)
    attention_local = lax.dynamic_slice_in_dim(attention_gain, blk_index * width_local, width_local)
    feedforward_local = lax.dynamic_slice_in_dim(
        feedforward_gain, blk_index * width_local, width_local
    )
    moved = move_caches(
        prompt_cache.reshape(group_per_device, pages_local * page_length, features), inverse
    )
    cache_here = moved.reshape(group_per_device, pages_local, page_length, features)
    owners = inverse[here]
    table_rows = page_table[owners, 0]
    owner_lengths = cache_lengths[owners]
    new_lengths = cache_lengths[inverse[here]]
    row_ids = jnp.arange(rows_per_device, dtype=jnp.int32)
    slice_ids = (
        jnp.arange(req_count, dtype=jnp.int32)[:, None] * blk_count + blk_index
    ) * slices_dev + jnp.arange(slices_dev, dtype=jnp.int32)[None, :]
    targets = (slice_ids // split_count).reshape(-1)
    slot_ids = jnp.arange(CAP, dtype=jnp.int32)
    tail_entries = []
    results = []
    for step_index in range(steps_count):
        current = step_inputs[step_index]
        if step_index > 0:
            parent_rows = row_ids // BEAMS * BEAMS + parents[step_index - 1]
            tail_entries = [
                (entry_pair[0][parent_rows], entry_pair[1][parent_rows])
                for entry_pair in tail_entries
            ]
        as_float = current.astype(jnp.float32)
        squares = lax.psum(jnp.sum(as_float * as_float, axis=1), "blk")
        normed_local = (
            as_float * lax.rsqrt(squares[:, None] / model_width + epsilon) * attention_local
        ).astype(jnp.bfloat16)
        shard_piece = lax.all_gather(normed_local, "blk", axis=1, tiled=True)
        query_local = jnp.dot(shard_piece, query_weight, preferred_element_type=jnp.float32)
        pair_local = jnp.dot(shard_piece, key_value_weight, preferred_element_type=jnp.float32)
        projected_q, key_value_projected = (
            lax.all_gather(query_local.astype(jnp.bfloat16), "blk", axis=1, tiled=True),
            lax.all_gather(pair_local.astype(jnp.bfloat16), "blk", axis=1, tiled=True),
        )
        position_list = jnp.repeat(new_lengths, group_of_rows) + step_index
        query_vectors = (
            apply_rotary(
                projected_q.astype(jnp.float32).reshape(rows_per_device, QUERY_HEADS, HEAD_WIDTH),
                position_list,
            )
            .astype(jnp.bfloat16)
            .reshape(rows_per_device, QUERY_HEADS * HEAD_WIDTH)
        )
        latest_keys = (
            apply_rotary(
                key_value_projected[:, : KEY_VALUE_HEADS * HEAD_WIDTH]
                .astype(jnp.float32)
                .reshape(rows_per_device, KEY_VALUE_HEADS, HEAD_WIDTH),
                position_list,
            )
            .astype(jnp.bfloat16)
            .reshape(rows_per_device, KEY_VALUE_HEADS * HEAD_WIDTH)
        )
        tail_entries = tail_entries + [
            (latest_keys, key_value_projected[:, KEY_VALUE_HEADS * HEAD_WIDTH :])
        ]
        recent_keys = jnp.stack([entry_pair[0] for entry_pair in tail_entries], axis=1)
        recent_values = jnp.stack([entry_pair[1] for entry_pair in tail_entries], axis=1)
        grouped_queries = query_vectors.reshape(
            group_per_device, group_of_rows, QUERY_HEADS * HEAD_WIDTH
        )
        score_peaks, softmax_totals, weighted_values = cache_partial(
            grouped_queries, cache_here, table_rows, owner_lengths, blk_index, blk_count
        )
        score_peaks = score_peaks.reshape(rows_per_device, QUERY_HEADS)
        softmax_totals = softmax_totals.reshape(rows_per_device, QUERY_HEADS)
        weighted_values = weighted_values.reshape(rows_per_device, QUERY_HEADS, HEAD_WIDTH)
        score_peaks, softmax_totals, weighted_values = joined(
            (score_peaks, softmax_totals, weighted_values), "blk", combine
        )
        heads = finish_heads(
            score_peaks, softmax_totals, weighted_values, query_vectors, recent_keys, recent_values
        )
        attention_out = jnp.dot(heads, output_weight, preferred_element_type=jnp.float32)
        attended = (current.astype(jnp.float32) + attention_out).astype(jnp.bfloat16)
        attended_float = attended.astype(jnp.float32)
        squares_h = lax.psum(jnp.sum(attended_float * attended_float, axis=1), "blk")
        normed_part = (
            attended_float
            * lax.rsqrt(squares_h[:, None] / model_width + epsilon)
            * feedforward_local
        ).astype(jnp.bfloat16)
        normed_h = lax.all_gather(normed_part, "blk", axis=1, tiled=True)
        logits = jnp.dot(normed_h, router_weight, preferred_element_type=jnp.float32)
        chosen = routes[step_index]
        raised = jnp.exp(jnp.take_along_axis(logits, chosen, axis=1))
        gate_weights = raised / jnp.sum(raised, axis=1, keepdims=True)
        flat_routes = chosen.reshape(-1)
        one_hot = (flat_routes[:, None] == jnp.arange(E, dtype=jnp.int32)[None, :]).astype(
            jnp.int32
        )
        ranks = jnp.sum((jnp.cumsum(one_hot, axis=0) - 1) * one_hot, axis=1)
        routes_first = chosen.T
        ranks_first = ranks.reshape(rows_per_device, TOPK).T
        matches = (routes_first[:, None, None, :] == targets[None, :, None, None]) & (
            ranks_first[:, None, None, :] == slot_ids[None, None, :, None]
        )
        dispatch = (
            jnp.any(matches, axis=0)
            .reshape(targets.shape[0] * CAP, rows_per_device)
            .astype(jnp.bfloat16)
        )
        sending = (
            jnp.dot(dispatch, normed_h, preferred_element_type=jnp.float32)
            .astype(jnp.bfloat16)
            .reshape(req_count, slices_dev, CAP, model_width)
        )
        mixing = jnp.sum(jnp.where(matches, gate_weights.T[:, None, None, :], 0.0), axis=0).reshape(
            targets.shape[0] * CAP, rows_per_device
        )
        mixing_high = mixing.astype(jnp.bfloat16)
        mixing_low = (mixing - mixing_high.astype(jnp.float32)).astype(jnp.bfloat16)
        arrived = lax.all_to_all(sending, "req", split_axis=0, concat_axis=0, tiled=True)
        gate_part = jnp.einsum(
            "sucd,udf->sucf", arrived, expert_gate, preferred_element_type=jnp.float32
        )
        up_part = jnp.einsum(
            "sucd,udf->sucf", arrived, expert_up, preferred_element_type=jnp.float32
        )
        hidden = (jax.nn.silu(gate_part) * up_part).astype(jnp.bfloat16)
        produced = jnp.einsum(
            "sucf,ufd->sucd", hidden, expert_down, preferred_element_type=jnp.float32
        ).astype(jnp.bfloat16)
        returned = lax.all_to_all(produced, "req", split_axis=0, concat_axis=0, tiled=True)
        returned_rows = returned.reshape(-1, model_width)
        routed = jnp.dot(
            mixing_high.T, returned_rows, preferred_element_type=jnp.float32
        ) + jnp.dot(mixing_low.T, returned_rows, preferred_element_type=jnp.float32)
        shared_act = (
            jax.nn.silu(jnp.dot(normed_h, shared_gate, preferred_element_type=jnp.float32))
            * jnp.dot(normed_h, shared_up, preferred_element_type=jnp.float32)
        ).astype(jnp.bfloat16)
        expert_terms = routed + jnp.dot(shared_act, shared_down, preferred_element_type=jnp.float32)
        summed = lax.psum_scatter(
            expert_terms.astype(jnp.bfloat16), "blk", scatter_dimension=1, tiled=True
        ).astype(jnp.float32)
        results.append((attended.astype(jnp.float32) + summed).astype(jnp.bfloat16))
    return jnp.stack(results, axis=0)


def solution(mesh):
    in_specs = (
        P(None, "req", "blk"),
        P(),
        P(None, "blk"),
        P(None, "blk"),
        P(None, "blk"),
        P("req", "blk", None, None),
        P(None, "blk", None),
        P(),
        P(),
        P(None, "req"),
        P(None, "req", None),
        P(),
        P(),
        P(("req", "blk"), None, None),
        P(("req", "blk"), None, None),
        P(("req", "blk"), None, None),
        P(None, "blk"),
        P(None, "blk"),
        P("blk", None),
    )
    out_specs = P(None, "req", "blk")
    return jax.shard_map(
        per_device, mesh=mesh, in_specs=in_specs, out_specs=out_specs, check_vma=False
    )
```

profile of v0, /device:TPU:0, one launch (start us, length us, event | category | flops | bytes accessed | tf_op | source)
XLA Modules:
  0.0 636.7 jit_solution(6009953301910145482)
XLA Ops:
  6.6 7.6 %all-to-all-start = ((bf16[1,8,192,1024]{3,2,0,1:T(8,128)(2,1)}), bf16[1,8,192,1024]{3,2,0,1:T(8,128)(2,1)}, u32[]{:S(2)}, u32[]{:S(2)}) async-start(bf16[1,8,192,1024]{3,2,0,1:T(8,128)(2,1)} %bitcast.506), calls=%async_computation | async-start | bytes 6291456 | tf_op jit(solution)/shard_map/all_to_all | solution.py:63
  21.4 6.7 %all-reduce.1 = (f32[64]{0:T(128)S(1)}, f32[64]{0:T(128)S(1)}) all-reduce(f32[64]{0:T(128)S(1)} %get-tuple-element.689, f32[64]{0:T(128)S(1)} %get-tuple-element.690), channel_id=1, replica_groups=mesh['req'=8,'blk'=4] {'blk'}, use_global_device_ids=true, to_apply=%region_2.3 | all-reduce | flops 128 | bytes 1024 | tf_op jit(solution)/shard_map/psum | solution.py:254
  28.9 6.0 all_gather.49
  37.2 5.4 all_gather.54
  44.1 6.4 %all_gather.42 = bf16[64,2560]{1,0:T(8,128)(2,1)S(1)} all-gather(bf16[64,640]{1,0:T(8,128)(2,1)} %get-tuple-element.799), channel_id=1, replica_groups=mesh['req'=8,'blk'=4] {'blk'}, dimensions={1}, use_global_device_ids=true | all-gather | bytes 409600 | tf_op jit(solution)/shard_map/all_gather | solution.py:258
  53.1 2.6 convolution_convert_fusion.2
  55.7 29.2 %all-to-all-done = bf16[1,8,192,1024]{3,2,0,1:T(8,128)(2,1)} async-done(((bf16[1,8,192,1024]{3,2,0,1:T(8,128)(2,1)}), bf16[1,8,192,1024]{3,2,0,1:T(8,128)(2,1)}, u32[]{:S(2)}, u32[]{:S(2)}) %all-to-all-start) | async-done | bytes 3145760 | tf_op jit(solution)/shard_map/all_to_all | solution.py:63
  84.9 4.4 gather_fusion
  89.3 4.0 fusion.58
  93.2 4.5 all-to-all-start.1
  97.8 6.6 %all_gather.50 = bf16[64,2560]{1,0:T(8,128)(2,1)} all-gather(bf16[64,640]{1,0:T(8,128)(2,1)S(1)} %convolution_convert_fusion.2), channel_id=1, replica_groups=mesh['req'=8,'blk'=4] {'blk'}, dimensions={1}, use_global_device_ids=true | all-gather | bytes 409600 | tf_op jit(solution)/shard_map/all_gather | solution.py:262
  104.3 2.1 reshape.838
  107.9 5.4 all_gather.47
  122.4 2.6 fusion.171
  128.8 2.7 convolution_convert_fusion.3
  131.6 6.9 %all_gather.43 = bf16[64,2560]{1,0:T(8,128)(2,1)} all-gather(bf16[64,640]{1,0:T(8,128)(2,1)S(1)} %convolution_convert_fusion.3), channel_id=1, replica_groups=mesh['req'=8,'blk'=4] {'blk'}, dimensions={1}, use_global_device_ids=true | all-gather | bytes 409600 | tf_op jit(solution)/shard_map/all_gather | solution.py:262
  155.9 12.0 %all-to-all-done.1 = bf16[1,8,192,1024]{3,2,0,1:T(8,128)(2,1)} async-done(((bf16[1,8,192,1024]{3,2,0,1:T(8,128)(2,1)}), bf16[1,8,192,1024]{3,2,0,1:T(8,128)(2,1)}, u32[]{:S(2)}, u32[]{:S(2)}) %all-to-all-start.1) | async-done | bytes 3145760 | tf_op jit(solution)/shard_map/all_to_all | solution.py:66
  167.9 4.7 copy.297
  173.5 38.2 %while.73 = (s32[]{:T(128)}, f32[1,64,4,5]{1,3,2,0:T(8,128)S(1)}, f32[1,64,4,5]{1,3,2,0:T(8,128)S(1)}, f32[1,64,4,5,128]{4,1,3,2,0:T(8,128)}, s32[]{:T(128)}, /*...) while((s32[]{:T(128)}, f32[1,64,4,5]{1,3,2,0:T(8,128)S(1)}, ...), condition=%wide.region_23.25_spmd, body=%wide.region_20.24_spmd.sunk | while | flops 85692424 | bytes 10240861 | solution.py:133
  212.6 35.8 %while.71 = (s32[]{:T(128)}, f32[1,64,4,5]{1,3,2,0:T(8,128)S(1)}, f32[1,64,4,5]{1,3,2,0:T(8,128)S(1)}, f32[1,64,4,5,128]{4,1,3,2,0:T(8,128)}, s32[]{:T(128)}, /*...) while((s32[]{:T(128)}, f32[1,64,4,5]{1,3,2,0:T(8,128)S(1)}, ...), condition=%wide.region_6.7_spmd, body=%wide.region_3.6_spmd.sunk | while | flops 85692424 | bytes 10240861 | solution.py:133
  248.5 5.7 all_gather.51
  254.1 5.7 all_gather.52
  259.8 5.2 all_gather.44
  265.0 5.5 all_gather.45
  271.9 17.8 %all-gather.5.cloned.1.call-done = f32[4,64,20,128]{3,1,2,0:T(8,128)} async-done(((f32[1,64,20,128]{3,1,2,0:T(8,128)}), f32[4,64,20,128]{3,1,2,0:T(8,128)}) %all-gather.5.cloned.1.call-update) | async-done | bytes 2621456 | tf_op jit(solution)/shard_map/all_gather | solution.py:22
  292.2 17.3 %while.74 = (s32[]{:T(128)}, f32[64,20]{0,1:T(8,128)S(1)}, f32[64,20]{0,1:T(8,128)S(1)}, f32[64,20,128]{2,1,0:T(8,128)}, f32[4,64,20]{1,2,0:T(8,128)}, /*index=5...) while((s32[]{:T(128)}, f32[64,20]{0,1:T(8,128)S(1)}, ...), condition=%wide.region_25.27_spmd, body=%wide.region_24.26_spmd.sunk | while | flops 499205 | bytes 3348631 | solution.py:27
  295.1 2.8 fusion.258
  300.9 2.8 fusion.258
  306.7 2.8 fusion.258
  309.5 2.1 copy.322
  312.4 2.1 fusion.118
  317.1 3.3 fusion.84
  320.4 2.1 reshape.713
  322.5 76.2 %all-gather.3.cloned.1.call-done = f32[4,64,20,128]{3,1,2,0:T(8,128)} async-done(((f32[1,64,20,128]{3,1,2,0:T(8,128)}), f32[4,64,20,128]{3,1,2,0:T(8,128)}) %all-gather.3.cloned.1.call-update) | async-done | bytes 2621456 | tf_op jit(solution)/shard_map/all_gather | solution.py:22
  401.1 15.0 %while.72 = (s32[]{:T(128)}, f32[64,20]{0,1:T(8,128)S(1)}, f32[64,20]{0,1:T(8,128)S(1)}, f32[64,20,128]{2,1,0:T(8,128)}, f32[4,64,20]{1,2,0:T(8,128)S(1)}, /*ind...) while((s32[]{:T(128)}, f32[64,20]{0,1:T(8,128)S(1)}, ...), condition=%wide.region_8.9_spmd, body=%wide.region_7.8_spmd.sunk | while | flops 499205 | bytes 3348631 | solution.py:27
  403.3 2.8 fusion.249
  408.3 2.8 fusion.249
  413.3 2.8 fusion.249
  416.1 2.1 copy.302
  422.4 2.1 reshape.700
  424.5 2.5 multiply_reduce_fusion
  427.8 5.9 all-reduce
  434.8 6.2 all_gather.55
  442.6 14.1 %all-to-all-start.4 = ((bf16[8,2,16,2560]{3,2,1,0:T(8,128)(2,1)}), bf16[8,2,16,2560]{3,2,1,0:T(8,128)(2,1)S(1)}, u32[]{:S(2)}, u32[]{:S(2)}) async-start(bf16[8,2,16,2560]{3,2,1,0:T(8,128)(2,1)} %bitcast.116), calls=%async_computation.4 | async-start | bytes 2621440 | tf_op jit(solution)/shard_map/all_to_all | solution.py:343
  459.3 2.9 gather_fusion.4
  462.4 6.0 all_gather.48
  468.6 2.9 gather_fusion.3
  473.6 15.0 %all-to-all-done.4 = bf16[8,2,16,2560]{3,2,1,0:T(8,128)(2,1)S(1)} async-done(((bf16[8,2,16,2560]{3,2,1,0:T(8,128)(2,1)}), bf16[8,2,16,2560]{3,2,1,0:T(8,128)(2,1)S(1)}, u32[]{:S(2)}, u32[]{:S(2)}) %all-to-all-start.4) | async-done | bytes 1310752 | tf_op jit(solution)/shard_map/all_to_all | solution.py:343
  488.7 4.1 all-to-all-start.2
  492.8 7.8 %fusion.62 = f32[8,2,16,1536]{3,2,0,1:T(8,128)S(1)} fusion(bf16[2,2560,1536]{2,1,0:T(8,128)(2,1)} %param.42, bf16[8,2,16,2560]{3,2,1,0:T(8,128)(2,1)S(1)} %all-to-all-done.4), kind=kOutput, calls=%fused_computation.94 | convolution fusion | flops 2013265920 | bytes 18612224 | tf_op jit(solution)/shard_map/sucd,udf->sucf/dot_general | solution.py:344
  500.7 8.2 %fusion.74 = bf16[8,2,16,1536]{3,2,0,1:T(8,128)(2,1)S(1)} fusion(bf16[2,2560,1536]{2,1,0:T(8,128)(2,1)} %param.43, f32[8,2,16,1536]{3,2,0,1:T(8,128)S(1)} %fusion.62, bf16[8,2,16,2560]{3,2,1,0:T(8,128)(2,1)S(1)} %all-to-all-done.4), kind=kOutput, calls=%fused_computation.98 | convolution fusion | flops 2015625216 | bytes 19398656 | tf_op jit(solution)/shard_map/sucd,udf->sucf/dot_general | solution.py:347
  508.9 2.2 fusion.50
  512.3 12.0 %all-to-all-done.2 = bf16[8,2,16,2560]{3,2,1,0:T(8,128)(2,1)S(1)} async-done(((bf16[8,2,16,2560]{3,2,1,0:T(8,128)(2,1)}), bf16[8,2,16,2560]{3,2,1,0:T(8,128)(2,1)S(1)}, u32[]{:S(2)}, u32[]{:S(2)}) %all-to-all-start.2) | async-done | bytes 1310752 | tf_op jit(solution)/shard_map/all_to_all | solution.py:343
  524.3 3.8 all-to-all-start.5
  528.2 7.8 %fusion.59 = f32[8,2,16,1536]{3,2,0,1:T(8,128)S(1)} fusion(bf16[2,2560,1536]{2,1,0:T(8,128)(2,1)} %param.42, bf16[8,2,16,2560]{3,2,1,0:T(8,128)(2,1)S(1)} %all-to-all-done.2), kind=kOutput, calls=%fused_computation.93 | convolution fusion | flops 2013265920 | bytes 18612224 | tf_op jit(solution)/shard_map/sucd,udf->sucf/dot_general | solution.py:344
  536.1 8.2 %fusion.80 = bf16[8,2,16,1536]{3,2,0,1:T(8,128)(2,1)S(1)} fusion(bf16[2,2560,1536]{2,1,0:T(8,128)(2,1)} %param.43, f32[8,2,16,1536]{3,2,0,1:T(8,128)S(1)} %fusion.59, bf16[8,2,16,2560]{3,2,1,0:T(8,128)(2,1)S(1)} %all-to-all-done.2), kind=kOutput, calls=%fused_computation.100 | convolution fusion | flops 2015625216 | bytes 19398656 | tf_op jit(solution)/shard_map/sucd,udf->sucf/dot_general | solution.py:347
  544.3 2.2 fusion.53
  547.7 12.0 %all-to-all-done.5 = bf16[8,2,16,2560]{3,2,1,0:T(8,128)(2,1)S(1)} async-done(((bf16[8,2,16,2560]{3,2,1,0:T(8,128)(2,1)}), bf16[8,2,16,2560]{3,2,1,0:T(8,128)(2,1)S(1)}, u32[]{:S(2)}, u32[]{:S(2)}) %all-to-all-start.5) | async-done | bytes 1310752 | tf_op jit(solution)/shard_map/all_to_all | solution.py:354
  560.8 3.6 all-to-all-start.3
  565.3 3.3 fusion.177
  571.8 5.2 fusion.57
  578.1 17.8 %all-to-all-done.3 = bf16[8,2,16,2560]{3,2,1,0:T(8,128)(2,1)S(1)} async-done(((bf16[8,2,16,2560]{3,2,1,0:T(8,128)(2,1)}), bf16[8,2,16,2560]{3,2,1,0:T(8,128)(2,1)S(1)}, u32[]{:S(2)}, u32[]{:S(2)}) %all-to-all-start.3) | async-done | bytes 1310752 | tf_op jit(solution)/shard_map/all_to_all | solution.py:354
  597.6 6.3 fusion.56
  608.6 18.1 %reduce-scatter.7.cloned.1.call-done = bf16[640,64]{1,0:T(8,128)(2,1)} async-done(((bf16[2560,64]{1,0:T(8,128)(2,1)}), bf16[640,64]{1,0:T(8,128)(2,1)}) %reduce-scatter.7.cloned.1.call-update) | async-done | bytes 81936
  (432 shorter events, 154.2 us)
Async XLA Ops:
  6.5 418.0 %copy-start = (bf16[2560,640]{1,0:T(8,128)(2,1)S(1)}, bf16[2560,640]{1,0:T(8,128)(2,1)}, u32[]{:S(2)}) copy-start(bf16[2560,640]{1,0:T(8,128)(2,1)} %param.33) | copy-start | bytes 9830404
  6.5 7.6 %copy-start.47 = (s32[8]{0:T(128)S(1)}, s32[8]{0:T(128)}, u32[]{:S(2)}) copy-start(s32[8]{0:T(128)} %param.37) | copy-start | bytes 100
  6.5 10.8 %copy-start.48 = (s32[8]{0:T(128)S(1)}, s32[8]{0:T(128)}, u32[]{:S(2)}) copy-start(s32[8]{0:T(128)} %param.36) | copy-start | bytes 100
  6.5 12.9 %copy-start.40 = (s32[2,64,6]{1,0,2:T(2,128)S(1)}, s32[2,64,6]{1,0,2:T(2,128)}, u32[]{:S(2)}) copy-start(s32[2,64,6]{1,0,2:T(2,128)} %param.39) | copy-start | bytes 9220
  6.5 14.8 %copy-start.18 = (bf16[2,64,640]{2,1,0:T(8,128)(2,1)S(1)}, bf16[2,64,640]{2,1,0:T(8,128)(2,1)}, u32[]{:S(2)}) copy-start(bf16[2,64,640]{2,1,0:T(8,128)(2,1)} %param.29) | copy-start | bytes 491524
  6.6 78.4 %all-to-all-start = ((bf16[1,8,192,1024]{3,2,0,1:T(8,128)(2,1)}), bf16[1,8,192,1024]{3,2,0,1:T(8,128)(2,1)}, u32[]{:S(2)}, u32[]{:S(2)}) async-start(bf16[1,8,192,1024]{3,2,0,1:T(8,128)(2,1)} %bitcast.506), calls=%async_computation | async-start | bytes 6291456 | tf_op jit(solution)/shard_map/all_to_all | solution.py:63
  43.3 9.7 %copy-start.13 = (bf16[64,2560]{1,0:T(8,128)(2,1)S(1)}, bf16[64,2560]{1,0:T(8,128)(2,1)}, u32[]{:S(2)}) copy-start(bf16[64,2560]{1,0:T(8,128)(2,1)} %copy-done.12) | copy-start | bytes 983044
  43.4 12.3 %copy-start.41 = (f32[64]{0:T(128)}, f32[64]{0:T(128)S(1)}, u32[]{:S(2)}) copy-start(f32[64]{0:T(128)S(1)} %get-tuple-element.827) | copy-start | bytes 772
  43.4 12.3 %copy-start.42 = (f32[64]{0:T(128)}, f32[64]{0:T(128)S(1)}, u32[]{:S(2)}) copy-start(f32[64]{0:T(128)S(1)} %get-tuple-element.828) | copy-start | bytes 772
  93.2 74.7 %all-to-all-start.1 = ((bf16[1,8,192,1024]{3,2,0,1:T(8,128)(2,1)}), bf16[1,8,192,1024]{3,2,0,1:T(8,128)(2,1)}, u32[]{:S(2)}, u32[]{:S(2)}) async-start(bf16[1,8,192,1024]{3,2,0,1:T(8,128)(2,1)} %fusion.58), calls=%async_computation.1 | async-start | bytes 6291456 | tf_op jit(solution)/shard_map/all_to_all | solution.py:66
  97.7 192.0 %all-gather.5.cloned.1.call-start = ((), (), s32[]{:S(2)}) async-start(), calls=%async_computation.9 | async-start | bytes 3276800 | tf_op jit(solution)/shard_map/all_gather | solution.py:22
  115.1 2.1 copy-start.43
  115.1 2.1 copy-start.45
  120.4 2.0 copy-start.30
  120.4 2.0 copy-start.31
  120.4 2.0 copy-start.32
  121.4 5.2 copy-start.27
  128.8 11.7 %copy-start.24 = (bf16[64,4,64]{2,1,0:T(4,128)(2,1)S(1)}, bf16[64,4,64]{2,1,0:T(4,128)(2,1)}, u32[]{:S(2)}) copy-start(bf16[64,4,64]{2,1,0:T(4,128)(2,1)} %copy-done.23) | copy-start | bytes 98308
  131.6 10.7 %copy-start.44 = (f32[64]{0:T(128)S(1)}, f32[64]{0:T(128)}, u32[]{:S(2)}) copy-start(f32[64]{0:T(128)} %copy-done.43) | copy-start | bytes 772
  131.6 10.7 %copy-start.46 = (f32[64]{0:T(128)S(1)}, f32[64]{0:T(128)}, u32[]{:S(2)}) copy-start(f32[64]{0:T(128)} %copy-done.45) | copy-start | bytes 772
  142.3 2.4 copy-start.25
  153.2 2.0 copy-start.36
  174.2 5.6 copy-start.4
  181.8 5.6 copy-start.4
  189.5 5.6 copy-start.4
  197.1 5.6 copy-start.4
  204.7 5.6 copy-start.4
  211.7 187.0 %all-gather.3.cloned.1.call-start = ((), (), s32[]{:S(2)}) async-start(), calls=%async_computation.8 | async-start | bytes 3276800 | tf_op jit(solution)/shard_map/all_gather | solution.py:22
  213.4 5.1 copy-start.2
  220.5 5.1 copy-start.2
  227.7 5.1 copy-start.2
  234.8 5.1 copy-start.2
  242.0 5.1 copy-start.2
  292.2 19.4 %copy-start.38 = (f32[64,4,5]{0,1,2:T(4,128)S(1)}, f32[64,4,5]{0,1,2:T(4,128)}, u32[]{:S(2)}) copy-start(f32[64,4,5]{0,1,2:T(4,128)} %copy.331) | copy-start | bytes 15364
  416.1 8.4 %copy-start.19 = (bf16[2,64,640]{2,1,0:T(8,128)(2,1)S(1)}, bf16[2,64,640]{2,1,0:T(8,128)(2,1)}, u32[]{:S(2)}) copy-start(bf16[2,64,640]{2,1,0:T(8,128)(2,1)} %param.29) | copy-start | bytes 491524
  424.5 2.5 copy-start.20
  424.5 2.5 copy-start.21
  427.0 6.7 %copy-start.39 = (f32[640]{0:T(1024)S(1)}, f32[640]{0:T(1024)}, u32[]{:S(2)}) copy-start(f32[640]{0:T(1024)} %dynamic_slice.97) | copy-start | bytes 7684
  427.0 14.0 %copy-start.29 = (pred[16,16,64]{2,1,0:T(8,128)(4,1)S(1)}, pred[16,16,64]{2,1,0:T(8,128)(4,1)}, u32[]{:S(2)}) copy-start(pred[16,16,64]{2,1,0:T(8,128)(4,1)} %and_reduce_fusion) | copy-start | bytes 49156
  433.8 23.6 %copy-start.26 = (s32[64,3,128]{2,0,1:T(8,128)S(1)}, s32[64,3,128]{2,0,1:T(8,128)}, u32[]{:S(2)}) copy-start(s32[64,3,128]{2,0,1:T(8,128)} %fusion.137) | copy-start | bytes 294916
  434.8 24.1 %copy-start.33 = (pred[6,16,64]{2,1,0:T(8,128)(4,1)S(1)}, pred[6,16,64]{2,1,0:T(8,128)(4,1)}, u32[]{:S(2)}) copy-start(pred[6,16,64]{2,1,0:T(8,128)(4,1)} %get-tuple-element.817) | copy-start | bytes 18436
  441.1 18.0 %copy-start.22 = (bf16[2560,64]{0,1:T(8,128)(2,1)S(1)}, bf16[2560,64]{0,1:T(8,128)(2,1)}, u32[]{:S(2)}) copy-start(bf16[2560,64]{0,1:T(8,128)(2,1)} %param.41) | copy-start | bytes 983044
  442.6 46.0 %all-to-all-start.4 = ((bf16[8,2,16,2560]{3,2,1,0:T(8,128)(2,1)}), bf16[8,2,16,2560]{3,2,1,0:T(8,128)(2,1)S(1)}, u32[]{:S(2)}, u32[]{:S(2)}) async-start(bf16[8,2,16,2560]{3,2,1,0:T(8,128)(2,1)} %bitcast.116), calls=%async_computation.4 | async-start | bytes 2621440 | tf_op jit(solution)/shard_map/all_to_all | solution.py:343
  468.4 3.6 copy-start.9
  468.6 3.2 copy-start.35
  468.6 3.2 copy-start.37
  488.7 35.7 %all-to-all-start.2 = ((bf16[8,2,16,2560]{3,2,1,0:T(8,128)(2,1)}), bf16[8,2,16,2560]{3,2,1,0:T(8,128)(2,1)S(1)}, u32[]{:S(2)}, u32[]{:S(2)}) async-start(bf16[8,2,16,2560]{3,2,1,0:T(8,128)(2,1)} %bitcast.505), calls=%async_computation.2 | async-start | bytes 2621440 | tf_op jit(solution)/shard_map/all_to_all | solution.py:343
  492.8 16.1 %slice-start = ((s8[15728640]{0:T(1024)(128)(4,1)}), s8[4194304]{0:T(1024)(128)(4,1)S(1)}, s32[]{:S(2)}) async-start(s8[15728640]{0:T(1024)(128)(4,1)} %bitcast.486), calls=%async_computation.12 | async-start | bytes 8388608
  492.8 16.1 %slice-start.1 = ((s8[15728640]{0:T(1024)(128)(4,1)}), s8[4194304]{0:T(1024)(128)(4,1)S(1)}, s32[]{:S(2)}) async-start(s8[15728640]{0:T(1024)(128)(4,1)} %bitcast.486), calls=%async_computation.13 | async-start | bytes 8388608
  500.6 8.2 %slice-start.2 = ((s8[15728640]{0:T(1024)(128)(4,1)}), s8[4194304]{0:T(1024)(128)(4,1)S(1)}, s32[]{:S(2)}) async-start(s8[15728640]{0:T(1024)(128)(4,1)} %bitcast.486), calls=%async_computation.14 | async-start | bytes 8388608
  500.7 8.2 %slice-start.3 = ((s8[15728640]{0:T(1024)(128)(4,1)}), s8[3145728]{0:T(1024)(128)(4,1)S(1)}, s32[]{:S(2)}) async-start(s8[15728640]{0:T(1024)(128)(4,1)} %bitcast.486), calls=%async_computation.15 | async-start | bytes 6291456
  524.3 35.4 %all-to-all-start.5 = ((bf16[8,2,16,2560]{3,2,1,0:T(8,128)(2,1)}), bf16[8,2,16,2560]{3,2,1,0:T(8,128)(2,1)S(1)}, u32[]{:S(2)}, u32[]{:S(2)}) async-start(bf16[8,2,16,2560]{3,2,1,0:T(8,128)(2,1)} %copy.350), calls=%async_computation.5 | async-start | bytes 2621440 | tf_op jit(solution)/shard_map/all_to_all | solution.py:354
  528.2 16.1 %slice-start.4 = ((s8[15728640]{0:T(1024)(128)(4,1)}), s8[4194304]{0:T(1024)(128)(4,1)S(1)}, s32[]{:S(2)}) async-start(s8[15728640]{0:T(1024)(128)(4,1)} %bitcast.488), calls=%async_computation.16 | async-start | bytes 8388608
  528.2 16.1 %slice-start.5 = ((s8[15728640]{0:T(1024)(128)(4,1)}), s8[4194304]{0:T(1024)(128)(4,1)S(1)}, s32[]{:S(2)}) async-start(s8[15728640]{0:T(1024)(128)(4,1)} %bitcast.488), calls=%async_computation.17 | async-start | bytes 8388608
  536.0 8.2 %slice-start.6 = ((s8[15728640]{0:T(1024)(128)(4,1)}), s8[4194304]{0:T(1024)(128)(4,1)S(1)}, s32[]{:S(2)}) async-start(s8[15728640]{0:T(1024)(128)(4,1)} %bitcast.488), calls=%async_computation.18 | async-start | bytes 8388608
  536.0 8.2 %slice-start.7 = ((s8[15728640]{0:T(1024)(128)(4,1)}), s8[3145728]{0:T(1024)(128)(4,1)S(1)}, s32[]{:S(2)}) async-start(s8[15728640]{0:T(1024)(128)(4,1)} %bitcast.488), calls=%async_computation.19 | async-start | bytes 6291456
  560.8 35.2 %all-to-all-start.3 = ((bf16[8,2,16,2560]{3,2,1,0:T(8,128)(2,1)}), bf16[8,2,16,2560]{3,2,1,0:T(8,128)(2,1)S(1)}, u32[]{:S(2)}, u32[]{:S(2)}) async-start(bf16[8,2,16,2560]{3,2,1,0:T(8,128)(2,1)} %copy.314), calls=%async_computation.3 | async-start | bytes 2621440 | tf_op jit(solution)/shard_map/all_to_all | solution.py:354
  564.4 41.5 %reduce-scatter.9.cloned.1.call-start = ((), (), s32[]{:S(2)}) async-start(), calls=%async_computation.11 | async-start | bytes 819200
  564.4 4.2 copy-start.6
  564.5 4.2 copy-start.10
  568.7 1.5 copy-start.8
  576.9 19.4 %copy-start.28 = (bf16[16,16,64]{2,1,0:T(8,128)(2,1)S(1)}, bf16[16,16,64]{2,1,0:T(8,128)(2,1)}, u32[]{:S(2)}) copy-start(bf16[16,16,64]{2,1,0:T(8,128)(2,1)} %get-tuple-element.775) | copy-start | bytes 98308
  578.1 48.6 %reduce-scatter.7.cloned.1.call-start = ((), (), s32[]{:S(2)}) async-start(), calls=%async_computation.10 | async-start | bytes 819200
  597.6 32.4 %copy-start.1 = (bf16[2560,640]{1,0:T(8,128)(2,1)S(1)}, bf16[2560,640]{1,0:T(8,128)(2,1)}, u32[]{:S(2)}) copy-start(bf16[2560,640]{1,0:T(8,128)(2,1)} %param.33) | copy-start | bytes 9830404
  (20 other events, 16.3 us)
Sparse Core Ops, SparseCore 0:
  211.8 77.8 all-gather.4
  291.3 107.3 all-gather.2
  578.2 22.9 reduce-scatter.8
  606.0 20.6 reduce-scatter.6
where the time goes:
time: 648 us; the launch traced here: 637 us
  waiting for transfers between devices  210 us (32%)
  local copies, waits for them, and re-layouts  111 us (17%)
  matrix products  96.3 us (15%)
  blocking collectives  83.5 us (13%)
  other arithmetic  59.5 us (9%)
  starting transfers between devices  37.9 us (6%)
  loops' own time  19.3 us (3%)
  between operations  18.4 us (3%)
    all_gather x2, waiting for transfers between devices, joined(): gathered = jax.tree.map(lambda a: lax.all_gather(a, axis), part)  94 us
    all_to_all x2, waiting for transfers between devices, per_device(): lax.all_to_all(produced, 'req', split_axis=0, concat_axis=0, tiled=True)  29.9 us
    all_to_all x1, waiting for transfers between devices, move_caches(): lax.all_to_all(pieces, 'req', split_axis=1, concat_axis=1, tiled=True)  29.2 us
    all_to_all x2, waiting for transfers between devices, per_device(): lax.all_to_all(sending, 'req', split_axis=0, concat_axis=0, tiled=True)  27.1 us
    all_gather x4, blocking collectives, joined(): gathered = jax.tree.map(lambda a: lax.all_gather(a, axis), part)  22 us
    another operation x2, loops' own time, cache_partial(): lax.fori_loop(0, visits, visit, initial)  19.3 us
    all_to_all x2, starting transfers between devices, per_device(): lax.all_to_all(sending, 'req', split_axis=0, concat_axis=0, tiled=True)  18.3 us
    unnamed x6, waiting for transfers between devices  18.2 us
  transfers between devices with their start and end apart: 10, of which 9 were waited for; matrix products, arithmetic and copies ran while one was open for 29% of the time, Pallas kernels for 0%

commit v1 on v0

v1 whole, which is shorter than its diff:
```python
import functools

import jax
import jax.numpy as jnp
from jax import lax
from jax.experimental import pallas as pl
from jax.experimental.pallas import tpu as pltpu
from jax.sharding import PartitionSpec as P

QUERY_HEADS = 20
KEY_VALUE_HEADS = 4
HEAD_WIDTH = 128
E = 64
FFE = 1536
TOPK = 6
BEAMS = 8
CAP = 16
GROUP = QUERY_HEADS // KEY_VALUE_HEADS

epsilon = 1e-05
rope_base = 500000.0
masked_floor = -1e30
MIB = 1 << 20


def push_kernel(axis, n, count, gather, *refs):
    ins, outs = refs[:count], refs[count : 2 * count]
    send_sem, recv_sem, local_sem = refs[2 * count :]
    me = lax.axis_index(axis)
    barrier = pltpu.get_barrier_semaphore()
    for k in range(1, n):
        pl.semaphore_signal(
            barrier,
            inc=1,
            device_id={axis: lax.rem(me + k, n)},
            device_id_type=pl.DeviceIdType.MESH,
        )
    pl.semaphore_wait(barrier, n - 1)
    copies = []
    for k in range(1, n):
        to = lax.rem(me + k, n)
        for i in range(count):
            copy = pltpu.make_async_remote_copy(
                src_ref=ins[i] if gather else ins[i].at[to],
                dst_ref=outs[i].at[me],
                send_sem=send_sem.at[i, k],
                recv_sem=recv_sem.at[i, k],
                device_id={axis: to},
                device_id_type=pl.DeviceIdType.MESH,
            )
            copy.start()
            copies.append(copy)
    own = []
    for i in range(count):
        copy = pltpu.make_async_copy(
            ins[i] if gather else ins[i].at[me], outs[i].at[me], local_sem.at[i]
        )
        copy.start()
        own.append(copy)
    for copy in own:
        copy.wait()
    for copy in copies:
        copy.wait()


def push(arrays, axis, collective_id, gather=False):
    n = lax.axis_size(axis)
    count = len(arrays)
    shapes = [
        jax.ShapeDtypeStruct(((n,) + a.shape) if gather else a.shape, a.dtype) for a in arrays
    ]
    return pl.pallas_call(
        functools.partial(push_kernel, axis, n, count, gather),
        out_shape=shapes,
        in_specs=[pl.BlockSpec(memory_space=pl.ANY)] * count,
        out_specs=[pl.BlockSpec(memory_space=pl.ANY)] * count,
        scratch_shapes=[
            pltpu.SemaphoreType.DMA((count, n)),
            pltpu.SemaphoreType.DMA((count, n)),
            pltpu.SemaphoreType.DMA((count,)),
        ],
        compiler_params=pltpu.CompilerParams(collective_id=collective_id, has_side_effects=True),
        name=f"push_{axis}_{collective_id}",
    )(*arrays)


def gather_columns(array, axis, collective_id):
    (blocks,) = push([array], axis, collective_id, gather=True)
    return jnp.transpose(blocks, (1, 0, 2)).reshape(array.shape[0], -1)


def permute_rows(rows, block_for, ids):
    n = lax.axis_size("req")
    pieces = rows.reshape(n, rows.shape[0] // n, rows.shape[1])
    (spread,) = push([pieces], "req", ids[0])
    (arrived,) = push([jnp.take(spread, block_for, axis=0)], "req", ids[1])
    return arrived.reshape(rows.shape)


def attention_kernel(
    tail_ref, q_ref, kv_ref, parent_ref, cos_ref, sin_ref, pos_ref, cache_ref, o_ref, lse_ref
):
    rows = q_ref.shape[0]
    scaling = HEAD_WIDTH ** (-0.5)
    key_width = KEY_VALUE_HEADS * HEAD_WIDTH
    cosines, sines = cos_ref[...], sin_ref[...]

    def rotated(block):
        block = block.astype(jnp.float32)
        half = HEAD_WIDTH // 2
        swapped = jnp.concatenate([block[:, half:], block[:, :half]], axis=1)
        return (block * cosines + swapped * sines).astype(jnp.bfloat16)

    tails_here = tail_ref[0] > 0
    valid = pos_ref[...] < tail_ref[1]
    parent = parent_ref[...]
    has_parent = jnp.sum(parent.astype(jnp.float32), axis=1, keepdims=True) > 0.5
    lse_ref[...] = jnp.full(lse_ref.shape, masked_floor, jnp.float32)
    for kv_head in range(KEY_VALUE_HEADS):
        keys_at = pl.ds(kv_head * HEAD_WIDTH, HEAD_WIDTH)
        values_at = pl.ds(key_width + kv_head * HEAD_WIDTH, HEAD_WIDTH)
        own_key = rotated(kv_ref[:, keys_at])
        own_value = kv_ref[:, values_at]
        parent_key = jnp.dot(parent, own_key, preferred_element_type=jnp.float32)
        parent_value = jnp.dot(parent, own_value, preferred_element_type=jnp.float32)
        own_key = own_key.astype(jnp.float32)
        own_value = own_value.astype(jnp.float32)
        keys = cache_ref[:, keys_at]
        values = cache_ref[:, values_at]
        for g in range(GROUP):
            head = kv_head * GROUP + g
            at = pl.ds(head * HEAD_WIDTH, HEAD_WIDTH)
            query = rotated(q_ref[:, at])
            scores = (
                lax.dot_general(
                    query, keys, (((1,), (1,)), ((), ())), preferred_element_type=jnp.float32
                )
                * scaling
            )
            query = query.astype(jnp.float32)
            own = jnp.sum(query * own_key, axis=1, keepdims=True) * scaling
            par = jnp.sum(query * parent_key, axis=1, keepdims=True) * scaling
            own = jnp.where(tails_here, own, masked_floor)
            par = jnp.where(has_parent & tails_here, par, masked_floor)
            scores = jnp.where(valid, scores, masked_floor)
            peak = jnp.maximum(jnp.max(scores, axis=1, keepdims=True), jnp.maximum(own, par))
            probs = jnp.where(valid, jnp.exp(scores - peak), 0.0)
            own = jnp.where(tails_here, jnp.exp(own - peak), 0.0)
            par = jnp.where(has_parent & tails_here, jnp.exp(par - peak), 0.0)
            total = jnp.sum(probs, axis=1, keepdims=True) + own + par
            weighted = jnp.dot(
                probs.astype(jnp.bfloat16), values, preferred_element_type=jnp.float32
            )
            weighted += own.astype(jnp.bfloat16).astype(jnp.float32) * own_value
            weighted += par.astype(jnp.bfloat16).astype(jnp.float32) * parent_value
            live = total > 0.0
            safe = jnp.where(live, total, 1.0)
            o_ref[:, at] = (weighted / safe).astype(jnp.bfloat16)
            lse_ref[:, head : head + 1] = jnp.where(live, peak + jnp.log(safe), masked_floor)


def attention_part(tail, q, kv, parent, cosines, sines, positions, cache):
    rows = q.shape[0]
    vmem = pl.BlockSpec(memory_space=pltpu.VMEM)
    return pl.pallas_call(
        attention_kernel,
        out_shape=[
            jax.ShapeDtypeStruct(q.shape, jnp.bfloat16),
            jax.ShapeDtypeStruct((rows, HEAD_WIDTH), jnp.float32),
        ],
        in_specs=[pl.BlockSpec(memory_space=pltpu.SMEM)] + [vmem] * 7,
        out_specs=[vmem] * 2,
        compiler_params=pltpu.CompilerParams(vmem_limit_bytes=40 * MIB),
        name="attention_part",
    )(tail, q, kv, parent, cosines, sines, positions, cache)


def merge_kernel(o_ref, lse_ref, out_ref):
    n = o_ref.shape[0]
    peaks = lse_ref[0]
    for b in range(1, n):
        peaks = jnp.maximum(peaks, lse_ref[b])
    scales = [jnp.exp(lse_ref[b] - peaks) for b in range(n)]
    total = scales[0]
    for b in range(1, n):
        total = total + scales[b]
    scales = [scale / total for scale in scales]
    for head in range(QUERY_HEADS):
        at = pl.ds(head * HEAD_WIDTH, HEAD_WIDTH)
        acc = o_ref[0, :, at].astype(jnp.float32) * scales[0][:, head : head + 1]
        for b in range(1, n):
            acc += o_ref[b, :, at].astype(jnp.float32) * scales[b][:, head : head + 1]
        out_ref[:, at] = acc.astype(jnp.bfloat16)


def merge(parts, lse):
    vmem = pl.BlockSpec(memory_space=pltpu.VMEM)
    return pl.pallas_call(
        merge_kernel,
        out_shape=jax.ShapeDtypeStruct(parts.shape[1:], jnp.bfloat16),
        in_specs=[vmem] * 2,
        out_specs=vmem,
        compiler_params=pltpu.CompilerParams(vmem_limit_bytes=40 * MIB),
        name="merge",
    )(parts, lse)


def norm_rows(values, gain):
    as_float = values.astype(jnp.float32)
    inverse = lax.rsqrt(jnp.mean(as_float * as_float, axis=-1, keepdims=True) + epsilon)
    return (as_float * inverse * gain).astype(jnp.bfloat16)


def inverse_of(migration):
    slot_ids = jnp.arange(migration.shape[0], dtype=jnp.int32)
    return jnp.sum(jnp.where(migration[None, :] == slot_ids[:, None], slot_ids[None, :], 0), axis=1)


def per_device(
    step_inputs,
    attention_gain,
    query_weight,
    key_value_weight,
    output_weight,
    prompt_cache,
    page_table,
    cache_lengths,
    migration,
    parents,
    routes,
    feedforward_gain,
    router_weight,
    expert_gate,
    expert_up,
    expert_down,
    shared_gate,
    shared_up,
    shared_down,
):
    n_req = lax.axis_size("req")
    n_blk = lax.axis_size("blk")
    req_index = lax.axis_index("req")
    blk_index = lax.axis_index("blk")
    steps, rows_dev, width_local = step_inputs.shape
    rows = steps * rows_dev
    _, pages_local, page_length, features = prompt_cache.shape
    model_width = width_local * n_blk
    slices_dev = expert_gate.shape[0]
    hidden_dev = expert_gate.shape[2]
    split_count = FFE // hidden_dev
    inverse = inverse_of(migration)

    here = step_inputs.reshape(rows, width_local)
    x_local = permute_rows(here, migration, (0, 1))
    all_parents = lax.all_gather(parents, "req")
    all_routes = lax.all_gather(routes, "req")
    my_parents = lax.dynamic_index_in_dim(all_parents, migration[req_index], 0, False)
    x = gather_columns(x_local, "blk", 2)
    normed_x = norm_rows(x, attention_gain)
    q_local = jnp.dot(normed_x, query_weight, preferred_element_type=jnp.float32)
    kv_local = jnp.dot(normed_x, key_value_weight, preferred_element_type=jnp.float32)
    q_blocks, kv_blocks = push(
        [q_local.astype(jnp.bfloat16), kv_local.astype(jnp.bfloat16)], "blk", 3, gather=True
    )
    q = jnp.transpose(q_blocks, (1, 0, 2)).reshape(rows, -1)
    kv = jnp.transpose(kv_blocks, (1, 0, 2)).reshape(rows, -1)

    length = cache_lengths[req_index]
    half = HEAD_WIDTH // 2
    frequency = rope_base ** (-2.0 * jnp.arange(half, dtype=jnp.float32) / HEAD_WIDTH)
    positions = length + jnp.arange(rows, dtype=jnp.int32) // rows_dev
    angles = positions.astype(jnp.float32)[:, None] * frequency
    cosines, sines = jnp.cos(angles), jnp.sin(angles)
    cosines = jnp.concatenate([cosines, cosines], axis=1)
    sines = jnp.concatenate([-sines, sines], axis=1)
    row_ids = jnp.arange(rows, dtype=jnp.int32)
    parent_rows = jnp.concatenate(
        [
            jnp.full((rows_dev,), -1, jnp.int32),
            jnp.arange(rows_dev, dtype=jnp.int32) // BEAMS * BEAMS + my_parents[0],
        ]
    )
    parent = (parent_rows[:, None] == row_ids[None, :]).astype(jnp.bfloat16)
    table = lax.dynamic_index_in_dim(page_table, req_index, 0, False)[0]
    local_ids = jnp.arange(pages_local, dtype=jnp.int32)
    logical = jnp.sum(jnp.where(table[None, :] == local_ids[:, None], local_ids[None, :], 0), axis=1)
    key_positions = (
        (logical * n_blk + blk_index)[:, None] * page_length
        + jnp.arange(page_length, dtype=jnp.int32)[None, :]
    ).reshape(1, -1)
    tail = jnp.stack([(blk_index == 0).astype(jnp.int32), length])
    part, lse = attention_part(
        tail,
        q,
        kv,
        parent,
        cosines,
        sines,
        key_positions,
        prompt_cache.reshape(pages_local * page_length, features),
    )
    share = rows // n_blk
    parts, lses = push(
        [part.reshape(n_blk, share, -1), lse.reshape(n_blk, share, HEAD_WIDTH)], "blk", 4
    )
    heads_mine = merge(parts, lses)
    (heads,) = push([heads_mine], "blk", 5, gather=True)
    heads = heads.reshape(rows, -1)
    attended_there = (
        x_local.astype(jnp.float32)
        + jnp.dot(heads, output_weight, preferred_element_type=jnp.float32)
    ).astype(jnp.bfloat16)
    attended_local = permute_rows(attended_there, inverse, (6, 7))
    attended = gather_columns(attended_local, "blk", 8)
    normed_h = norm_rows(attended, feedforward_gain)

    slice_ids = (
        jnp.arange(n_req, dtype=jnp.int32)[:, None] * n_blk + blk_index
    ) * slices_dev + jnp.arange(slices_dev, dtype=jnp.int32)[None, :]
    targets = slice_ids // split_count
    chosen = routes.reshape(rows, TOPK)
    named = jnp.any(chosen[:, :, None] == jnp.arange(E, dtype=jnp.int32), axis=1)
    logits = jnp.dot(normed_h, router_weight, preferred_element_type=jnp.float32)
    raised = jnp.where(named, jnp.exp(jnp.where(named, logits, 0.0)), 0.0)
    gates = raised / jnp.sum(raised, axis=1, keepdims=True)
    match = jnp.any(chosen[None, None] == targets[:, :, None, None], axis=-1)
    places = jnp.cumsum(
        match.reshape(n_req, slices_dev * rows).astype(jnp.int32), axis=1
    ).reshape(match.shape)
    places = jnp.where(match, places - 1, -1)
    my_targets = targets[req_index]
    arriving = jnp.sum(
        jnp.any(
            all_routes.reshape(n_req, rows, TOPK)[:, None]
            == my_targets[None, :, None, None],
            axis=-1,
        ).astype(jnp.int32),
        axis=2,
    )
    ends = jnp.cumsum(arriving, axis=1)
    starts = ends - arriving
    expert_of = (targets[:, :, None] == jnp.arange(E, dtype=jnp.int32)).astype(jnp.float32)
    gate_of = jnp.einsum(
        "rje,ie->rji", expert_of, gates, precision=lax.Precision.HIGHEST
    )

    def experts(room):
        slots = jnp.arange(room, dtype=jnp.int32)
        taken = places[:, None] == slots[None, :, None, None]
        dispatch = jnp.any(taken, axis=2).reshape(n_req * room, rows).astype(jnp.bfloat16)
        mixing = jnp.sum(jnp.where(taken, gate_of[:, None], 0.0), axis=2).reshape(
            n_req * room, rows
        )
        sending = (
            jnp.dot(dispatch, normed_h, preferred_element_type=jnp.float32)
            .astype(jnp.bfloat16)
            .reshape(n_req, room, model_width)
        )
        (arrived,) = push([sending], "req", 9)
        members = arrived.reshape(n_req * room, model_width)
        mine = (
            (slots[None, :, None] >= starts[:, None]) & (slots[None, :, None] < ends[:, None])
        ).reshape(n_req * room, slices_dev)
        produced = jnp.zeros((n_req * room, model_width), jnp.float32)
        for j in range(slices_dev):
            gate_part = jnp.dot(members, expert_gate[j], preferred_element_type=jnp.float32)
            up_part = jnp.dot(members, expert_up[j], preferred_element_type=jnp.float32)
            hidden = jnp.where(
                mine[:, j : j + 1], jax.nn.silu(gate_part) * up_part, 0.0
            ).astype(jnp.bfloat16)
            produced += jnp.dot(hidden, expert_down[j], preferred_element_type=jnp.float32)
        (returned,) = push(
            [produced.astype(jnp.bfloat16).reshape(n_req, room, model_width)], "req", 10
        )
        returned = returned.reshape(n_req * room, model_width)
        high = mixing.astype(jnp.bfloat16)
        low = (mixing - high.astype(jnp.float32)).astype(jnp.bfloat16)
        return jnp.dot(high.T, returned, preferred_element_type=jnp.float32) + jnp.dot(
            low.T, returned, preferred_element_type=jnp.float32
        )

    routed = experts(slices_dev * steps * CAP)
    shared_act = (
        jax.nn.silu(jnp.dot(normed_h, shared_gate, preferred_element_type=jnp.float32))
        * jnp.dot(normed_h, shared_up, preferred_element_type=jnp.float32)
    ).astype(jnp.bfloat16)
    terms = routed + jnp.dot(shared_act, shared_down, preferred_element_type=jnp.float32)
    blocks = jnp.transpose(
        terms.astype(jnp.bfloat16).reshape(rows, n_blk, width_local), (1, 0, 2)
    )
    (blocks,) = push([blocks], "blk", 11)
    summed = jnp.sum(blocks.astype(jnp.float32), axis=0)
    out = (attended_local.astype(jnp.float32) + summed).astype(jnp.bfloat16)
    return out.reshape(steps, rows_dev, width_local)


def solution(mesh):
    in_specs = (
        P(None, "req", "blk"),
        P(),
        P(None, "blk"),
        P(None, "blk"),
        P(None, "blk"),
        P("req", "blk", None, None),
        P(None, "blk", None),
        P(),
        P(),
        P(None, "req"),
        P(None, "req", None),
        P(),
        P(),
        P(("req", "blk"), None, None),
        P(("req", "blk"), None, None),
        P(("req", "blk"), None, None),
        P(None, "blk"),
        P(None, "blk"),
        P("blk", None),
    )
    out_specs = P(None, "req", "blk")
    return jax.shard_map(
        per_device, mesh=mesh, in_specs=in_specs, out_specs=out_specs, check_vma=False
    )
```

time: 648 us -> 398 us (0.61)
  the two profiles are of different devices: /device:TPU:0 before, /device:TPU:9 now
where the time goes in v1:
time: 398 us; the launch traced here: 396 us
  Pallas kernels  234 us (59%)
  matrix products  73.5 us (18%)
  blocking collectives  36.9 us (9%)
  local copies, waits for them, and re-layouts  27.6 us (7%)
  other arithmetic  21.5 us (5%)
    pallas_call x12, Pallas kernels, push(): pl.pallas_call(functools.partial(push_kernel, axis, n, count, gather), ou...  223 us
    dot_general x2, matrix products, experts(): jnp.dot(hidden, expert_down[j], preferred_element_type=jnp.float32)  35 us
    all_gather x1, blocking collectives, per_device(): all_routes = lax.all_gather(routes, 'req')  22.2 us
    dot_general x2, matrix products, experts(): jnp.dot(members, expert_gate[j], preferred_element_type=jnp.float32)  18.3 us
    all_gather x1, blocking collectives, per_device(): all_parents = lax.all_gather(parents, 'req')  14.7 us
    pallas_call x1, Pallas kernels, attention_part(): pl.pallas_call(attention_kernel, out_shape=[jax.ShapeDtypeStruct(q.shape,...  10.9 us

profile of v1, /device:TPU:9, one launch (start us, length us, event | category | flops | bytes accessed | tf_op | source)
XLA Modules:
  0.0 396.0 jit_solution(14535584963154430896)
XLA Ops:
  0.2 0.9 eq.126
  1.2 0.6 reduce-window.6
  2.1 0.7 fusion.57
  2.8 1.2 dynamic_slice.17
  4.1 0.7 pad_add_fusion.tail_ref
  4.8 8.1 %push_req_0.1 = bf16[8,16,640]{2,1,0:T(8,128)(2,1)} custom-call(bf16[8,16,640]{2,1,0:T(8,128)(2,1)} %bitcast.161), custom_call_target="tpu_custom_call" | custom-call | tf_op jit(solution)/shard_map/push_req_0/pallas_call | solution.py:72
  12.9 0.8 select_reduce_fusion.2
  13.6 1.2 compare_select_fusion
  14.8 1.5 gather_fusion
  16.3 1.2 compare_and_fusion.1
  17.5 0.8 broadcast_select_fusion.1.refs_0_
  18.3 5.5 %push_req_1.1 = bf16[8,16,640]{2,1,0:T(8,128)(2,1)} custom-call(bf16[8,16,640]{2,1,0:T(8,128)(2,1)} %broadcast_select_fusion.1.refs_0_), custom_call_target="tpu_custom_call" | custom-call | tf_op jit(solution)/shard_map/push_req_1/pallas_call | solution.py:72
  23.8 13.0 %push_blk_2.1 = bf16[4,128,640]{2,1,0:T(8,128)(2,1)} custom-call(bf16[128,640]{1,0:T(8,128)(2,1)} %bitcast.152), custom_call_target="tpu_custom_call" | custom-call | tf_op jit(solution)/shard_map/push_blk_2/pallas_call | solution.py:72
  36.8 2.3 convert_bitcast_fusion.1
  39.0 2.8 copy.69
  41.8 1.3 fusion.44
  43.2 1.8 fusion.51
  45.0 1.4 convolution_convert_fusion.1.refs_0_
  46.4 1.0 convolution_convert_fusion.2.refs_1_
  47.5 12.8 %push_blk_3.1 = (bf16[4,128,640]{2,1,0:T(8,128)(2,1)}, bf16[4,128,256]{2,1,0:T(8,128)(2,1)}) custom-call(bf16[128,640]{1,0:T(8,128)(2,1)} %convolution_convert_fusion.1.refs_0_, bf16[128,256]{1,0:T(8,128)(2,1)} %convolution_convert_fusion.2.refs_1_), custom_call_target="tpu_custom_call" | custom-call | tf_op jit(solution)/shard_map/push_blk_3/pallas_call | solution.py:72
  60.2 2.0 copy.82
  62.2 1.0 copy.83
  63.2 14.7 %all-gather.2 = s32[8,1,64]{2,1,0:T(1,128)S(1)} all-gather(s32[1,1,64]{2,1,0:T(1,128)S(1)} %bitcast.162), channel_id=2, replica_groups=mesh['req'=8,'blk'=4] {'req'}, dimensions={0}, use_global_device_ids=true | all-gather | bytes 2304 | tf_op jit(solution)/shard_map/all_gather | solution.py:255
  80.6 0.6 fusion.81
  81.7 0.7 fusion.77
  82.6 1.1 copy-done.3
  83.7 10.9 %attention_part.1 = (bf16[128,2560]{1,0:T(8,128)(2,1)S(1)}, f32[128,128]{1,0:T(8,128)S(1)}) custom-call(s32[2]{0:T(128)S(1)} %pad_add_fusion.tail_ref, bf16[128,2560]{1,0:T(8,128)(2,1)S(1)} %bitcast.137, bf16[128,1024]{1,0:T(8,128)(2,1)S(1)} %bitcast.138, bf16[128,128]{1,0:T(8,128)(2,1)S(1)} %fusion.68.parent_ref, f32[128,128]{1,0:T(8,128)S(1)} %get-tuple-element.29.cos_ref, ...), custom_call_target="tpu_custom_call" | custom-call | tf_op jit(solution)/shard_map/attention_part/pallas_call | solution.py:165
  94.6 0.8 copy-done.4
  95.4 0.6 copy-done.8
  96.1 14.0 %push_blk_4.1 = (bf16[4,32,2560]{2,1,0:T(8,128)(2,1)}, f32[4,32,128]{2,1,0:T(8,128)}) custom-call(bf16[4,32,2560]{2,1,0:T(8,128)(2,1)} %bitcast.139, f32[4,32,128]{2,1,0:T(8,128)} %bitcast.140), custom_call_target="tpu_custom_call" | custom-call | tf_op jit(solution)/shard_map/push_blk_4/pallas_call | solution.py:72
  110.1 1.1 copy-done.5
  111.1 0.8 copy-done.7
  112.5 0.7 copy-done.6
  113.1 9.9 %push_blk_5.1 = bf16[4,32,2560]{2,1,0:T(8,128)(2,1)} custom-call(bf16[32,2560]{1,0:T(8,128)(2,1)} %copy-done.6), custom_call_target="tpu_custom_call" | custom-call | tf_op jit(solution)/shard_map/push_blk_5/pallas_call | solution.py:72
  123.0 3.5 fusion.53
  126.4 9.0 %push_req_6.1 = bf16[8,16,640]{2,1,0:T(8,128)(2,1)} custom-call(bf16[8,16,640]{2,1,0:T(8,128)(2,1)} %bitcast.157), custom_call_target="tpu_custom_call" | custom-call | tf_op jit(solution)/shard_map/push_req_6/pallas_call | solution.py:72
  135.5 1.5 gather_fusion.1
  137.0 0.8 broadcast_select_fusion.refs_0_
  137.8 6.6 %push_req_7.1 = bf16[8,16,640]{2,1,0:T(8,128)(2,1)} custom-call(bf16[8,16,640]{2,1,0:T(8,128)(2,1)} %broadcast_select_fusion.refs_0_), custom_call_target="tpu_custom_call" | custom-call | tf_op jit(solution)/shard_map/push_req_7/pallas_call | solution.py:72
  144.4 10.9 %push_blk_8.1 = bf16[4,128,640]{2,1,0:T(8,128)(2,1)} custom-call(bf16[128,640]{1,0:T(8,128)(2,1)} %bitcast.154), custom_call_target="tpu_custom_call" | custom-call | tf_op jit(solution)/shard_map/push_blk_8/pallas_call | solution.py:72
  155.3 1.3 fusion.45
  156.6 1.3 fusion.56
  158.3 2.4 convolution_convert_fusion
  160.7 59.5 %push_req_9.1 = bf16[8,64,2560]{2,1,0:T(8,128)(2,1)} custom-call(bf16[8,64,2560]{2,1,0:T(8,128)(2,1)} %bitcast.142), custom_call_target="tpu_custom_call" | custom-call | tf_op jit(solution)/shard_map/push_req_9/pallas_call | solution.py:72
  220.3 10.0 %fusion.4 = f32[512,1536]{1,0:T(8,128)} fusion(bf16[512,2560]{1,0:T(8,128)(2,1)} %bitcast.144, bf16[2,2560,1536]{2,1,0:T(8,128)(2,1)} %param.34), kind=kOutput, calls=%fused_computation.6 | convolution fusion | flops 4026531840 | bytes 13631488 | tf_op jit(solution)/shard_map/dot_general | solution.py:366
  230.3 22.2 %all-gather.1 = s32[16,64,6]{1,2,0:T(8,128)S(1)} all-gather(s32[2,64,6]{1,2,0:T(8,128)S(1)} %copy.77), channel_id=3, replica_groups=mesh['req'=8,'blk'=4] {'req'}, dimensions={0}, use_global_device_ids=true | all-gather | bytes 27648 | tf_op jit(solution)/shard_map/all_gather | solution.py:256
  252.6 0.7 fusion.78
  254.0 17.1 %fusion = f32[512,2560]{1,0:T(8,128)} fusion(bf16[2,1536,2560]{2,1,0:T(8,128)(2,1)} %param.36, bf16[512,2560]{1,0:T(8,128)(2,1)S(1)} %bitcast.145, bf16[2,2560,1536]{2,1,0:T(8,128)(2,1)} %param.35, f32[512,1536]{1,0:T(8,128)} %fusion.4, pred[512]{0:T(512)(128)(4,1)S(1)} %get-tuple-element.19), kind=kOutput, calls=%fused_computation.2 | convolution fusion | flops 8058568704 | bytes 26739200 | tf_op jit(solution)/shard_map/dot_general | solution.py:371
  271.1 8.2 %fusion.10 = f32[512,1536]{1,0:T(8,128)} fusion(bf16[512,2560]{1,0:T(8,128)(2,1)S(1)} %bitcast.146, bf16[2,2560,1536]{2,1,0:T(8,128)(2,1)} %param.34), kind=kOutput, calls=%fused_computation.12 | convolution fusion | flops 4026531840 | bytes 13631488 | tf_op jit(solution)/shard_map/dot_general | solution.py:366
  279.3 17.9 %add_convert_fusion = bf16[512,2560]{1,0:T(8,128)(2,1)} fusion(f32[512,2560]{1,0:T(8,128)} %fusion, bf16[2,1536,2560]{2,1,0:T(8,128)(2,1)} %param.36, bf16[512,2560]{1,0:T(8,128)(2,1)S(1)} %bitcast.147, bf16[2,2560,1536]{2,1,0:T(8,128)(2,1)} %param.35, f32[512,1536]{1,0:T(8,128)} %fusion.10, pred[512]{0:T(512)(128)(4,1)S(1)} %get-tuple-element.18), kind=kOutput, calls=%fused_computation.20 | convolution fusion | flops 8061190144 | bytes 29360640 | tf_op jit(solution)/shard_map/dot_general | solution.py:371
  297.2 57.4 %push_req_10.1 = bf16[8,64,2560]{2,1,0:T(8,128)(2,1)} custom-call(bf16[8,64,2560]{2,1,0:T(8,128)(2,1)} %bitcast.148), custom_call_target="tpu_custom_call" | custom-call | tf_op jit(solution)/shard_map/push_req_10/pallas_call | solution.py:72
  354.6 1.2 convert_bitcast_fusion
  355.8 3.0 copy.75
  358.7 1.7 fusion.49
  360.4 1.5 fusion.87
  362.8 1.6 fusion.20
  364.4 1.0 copy-done.12
  365.3 1.5 fusion.88
  366.8 6.7 %fusion.21 = bf16[128,2560]{1,0:T(8,128)(2,1)} fusion(f32[128,2560]{1,0:T(8,128)} %fusion.20, bf16[768,2560]{1,0:T(8,128)(2,1)} %param.39, bf16[128,2560]{0,1:T(8,128)(2,1)} %copy-done.11, bf16[2560,768]{1,0:T(8,128)(2,1)} %param.38, f32[128,768]{1,0:T(8,128)} %fusion.88), kind=kOutput, calls=%fused_computation.26 | convolution fusion | flops 1007878144 | bytes 10878976 | tf_op jit(solution)/shard_map/dot_general | solution.py:387
  373.5 2.2 copy.80
  375.7 2.2 copy.81
  377.9 16.2 %push_blk_11.1 = bf16[4,128,640]{2,1,0:T(8,128)(2,1)} custom-call(bf16[4,128,640]{2,1,0:T(8,128)(2,1)} %bitcast.150), custom_call_target="tpu_custom_call" | custom-call | tf_op jit(solution)/shard_map/push_blk_11/pallas_call | solution.py:72
  394.0 1.2 convert_reduce_fusion
  395.3 0.7 fusion.63
  (95 shorter events, 4.5 us)
Async XLA Ops:
  0.0 45.0 %copy-start = (bf16[2560,640]{1,0:T(8,128)(2,1)S(1)}, bf16[2560,640]{1,0:T(8,128)(2,1)}, u32[]{:S(2)}) copy-start(bf16[2560,640]{1,0:T(8,128)(2,1)} %param.23) | copy-start | bytes 9830404
  0.1 1.1 copy-start.19
  0.2 1.0 copy-start.21
  18.3 24.9 %copy-start.20 = (f32[2560]{0:T(1024)S(1)}, f32[2560]{0:T(1024)}, u32[]{:S(2)}) copy-start(f32[2560]{0:T(1024)} %param.22) | copy-start | bytes 30724
  43.1 3.3 copy-start.15
  46.4 16.8 %copy-start.26 = (s32[1,64]{1,0:T(1,128)S(1)}, s32[1,64]{1,0:T(1,128)}, u32[]{:S(2)}) copy-start(s32[1,64]{1,0:T(1,128)} %param.30) | copy-start | bytes 772
  46.4 31.5 %copy-start.25 = (s32[8]{0:T(128)S(1)}, s32[8]{0:T(128)}, u32[]{:S(2)}) copy-start(s32[8]{0:T(128)} %param.29) | copy-start | bytes 100
  46.4 36.2 %copy-start.2 = (bf16[1,12,128,1024]{3,2,1,0:T(8,128)(2,1)S(1)}, bf16[1,12,128,1024]{3,2,1,0:T(8,128)(2,1)}, u32[]{:S(2)}) copy-start(bf16[1,12,128,1024]{3,2,1,0:T(8,128)(2,1)} %param.26) | copy-start | bytes 9437188
  82.6 1.1 copy-start.3
  94.6 0.8 copy-start.4
  95.4 0.6 copy-start.8
  110.0 1.1 copy-start.5
  111.1 0.8 copy-start.7
  112.0 23.5 %copy-start.24 = (s32[8]{0:T(128)S(1)}, s32[8]{0:T(128)}, u32[]{:S(2)}) copy-start(s32[8]{0:T(128)} %get-tuple-element.25) | copy-start | bytes 100
  112.0 25.0 %copy-start.23 = (pred[8]{0:T(512)(128)(4,1)S(1)}, pred[8]{0:T(512)(128)(4,1)}, u32[]{:S(2)}) copy-start(pred[8]{0:T(512)(128)(4,1)} %get-tuple-element.27) | copy-start | bytes 28
  112.4 0.7 copy-start.6
  123.0 32.3 %copy-start.17 = (f32[2560]{0:T(1024)S(1)}, f32[2560]{0:T(1024)}, u32[]{:S(2)}) copy-start(f32[2560]{0:T(1024)} %param.32) | copy-start | bytes 30724
  126.4 31.9 %copy-start.16 = (pred[8,64,128]{2,1,0:T(8,128)(4,1)S(1)}, pred[8,64,128]{2,1,0:T(8,128)(4,1)}, u32[]{:S(2)}) copy-start(pred[8,64,128]{2,1,0:T(8,128)(4,1)} %fusion.57) | copy-start | bytes 196612
  220.2 10.1 %copy-start.18 = (s32[2,64,6]{1,0,2:T(2,128)S(1)}, s32[2,64,6]{1,0,2:T(2,128)}, u32[]{:S(2)}) copy-start(s32[2,64,6]{1,0,2:T(2,128)} %param.31) | copy-start | bytes 9220
  220.2 33.7 %copy-start.13 = (bf16[8,64,2560]{2,1,0:T(8,128)(2,1)S(1)}, bf16[8,64,2560]{2,1,0:T(8,128)(2,1)}, u32[]{:S(2)}) copy-start(bf16[8,64,2560]{2,1,0:T(8,128)(2,1)} %push_req_9.1) | copy-start | bytes 7864324
  297.2 57.4 %copy-start.10 = (bf16[4,128,640]{2,1,0:T(8,128)(2,1)S(1)}, bf16[4,128,640]{2,1,0:T(8,128)(2,1)}, u32[]{:S(2)}) copy-start(bf16[4,128,640]{2,1,0:T(8,128)(2,1)} %push_blk_8.1) | copy-start | bytes 1966084
  355.7 6.2 %copy-start.22 = (s32[8,2]{0,1:T(2,128)S(1)}, s32[8,2]{0,1:T(2,128)}, u32[]{:S(2)}) copy-start(s32[8,2]{0,1:T(2,128)} %copy-done.21) | copy-start | bytes 196
  355.7 6.5 %copy-start.9 = (bf16[8,64,2560]{2,1,0:T(8,128)(2,1)S(1)}, bf16[8,64,2560]{2,1,0:T(8,128)(2,1)}, u32[]{:S(2)}) copy-start(bf16[8,64,2560]{2,1,0:T(8,128)(2,1)} %push_req_10.1) | copy-start | bytes 7864324
  360.4 3.9 copy-start.11
  362.7 2.6 copy-start.12
  366.8 29.1 %copy-start.1 = (bf16[2560,640]{1,0:T(8,128)(2,1)S(1)}, bf16[2560,640]{1,0:T(8,128)(2,1)}, u32[]{:S(2)}) copy-start(bf16[2560,640]{1,0:T(8,128)(2,1)} %param.23) | copy-start | bytes 9830404
  373.5 21.8 %copy-start.14 = (bf16[8,16,640]{2,1,0:T(8,128)(2,1)S(1)}, bf16[8,16,640]{2,1,0:T(8,128)(2,1)}, u32[]{:S(2)}) copy-start(bf16[8,16,640]{2,1,0:T(8,128)(2,1)} %push_req_7.1) | copy-start | bytes 491524

commit v2 on v1

--- a/solution.py
+++ b/solution.py
@@ -41,7 +41,7 @@
         to = lax.rem(me + k, n)
         for i in range(count):
             copy = pltpu.make_async_remote_copy(
-                src_ref=ins[i] if gather else ins[i].at[to],
+                src_ref=ins[i] if gather[i] else ins[i].at[to],
                 dst_ref=outs[i].at[me],
                 send_sem=send_sem.at[i, k],
                 recv_sem=recv_sem.at[i, k],
@@ -53,7 +53,7 @@
     own = []
     for i in range(count):
         copy = pltpu.make_async_copy(
-            ins[i] if gather else ins[i].at[me], outs[i].at[me], local_sem.at[i]
+            ins[i] if gather[i] else ins[i].at[me], outs[i].at[me], local_sem.at[i]
         )
         copy.start()
         own.append(copy)
@@ -66,8 +66,11 @@
 def push(arrays, axis, collective_id, gather=False):
     n = lax.axis_size(axis)
     count = len(arrays)
+    if not isinstance(gather, tuple):
+        gather = (gather,) * count
     shapes = [
-        jax.ShapeDtypeStruct(((n,) + a.shape) if gather else a.shape, a.dtype) for a in arrays
+        jax.ShapeDtypeStruct(((n,) + a.shape) if whole else a.shape, a.dtype)
+        for a, whole in zip(arrays, gather)
     ]
     return pl.pallas_call(
         functools.partial(push_kernel, axis, n, count, gather),
@@ -89,12 +92,166 @@
     return jnp.transpose(blocks, (1, 0, 2)).reshape(array.shape[0], -1)
 
 
-def permute_rows(rows, block_for, ids):
+def permute_rows(rows, block_for, ids, beside=()):
     n = lax.axis_size("req")
     pieces = rows.reshape(n, rows.shape[0] // n, rows.shape[1])
-    (spread,) = push([pieces], "req", ids[0])
+    spread, *gathered = push(
+        [pieces, *beside], "req", ids[0], gather=(False,) + (True,) * len(beside)
+    )
     (arrived,) = push([jnp.take(spread, block_for, axis=0)], "req", ids[1])
-    return arrived.reshape(rows.shape)
+    return (arrived.reshape(rows.shape), *gathered)
+
+
+def experts_kernel(
+    n, sending, gate_hbm, up_hbm, down_hbm, high_ref, low_ref, shared_ref, out_ref,
+    gate, up, down, held, hidden, back, weight_sem, send_sem, recv_sem, home_sem, back_sem, own_sem,
+):
+    me = lax.axis_index("req")
+    near = n // 2
+    mine = lax.rem(me, near)
+    base = me - mine
+    other = lax.rem(base + near, n)
+
+    def target(i):
+        return (base if i < near else other) + lax.rem(mine + i % near, near)
+
+    def source(i):
+        return (base if i < near else other) + lax.rem(mine + near - i % near, near)
+
+    slices, _, width = gate.shape
+    room = held.shape[1] // slices
+    weights = []
+    for j in range(slices):
+        for number, (hbm, vmem) in enumerate(((gate_hbm, gate), (up_hbm, up), (down_hbm, down))):
+            copy = pltpu.make_async_copy(hbm.at[j], vmem.at[j], weight_sem.at[3 * j + number])
+            copy.start()
+            weights.append(copy)
+
+    barrier = pltpu.get_barrier_semaphore()
+    for k in range(1, n):
+        pl.semaphore_signal(
+            barrier,
+            inc=1,
+            device_id={"req": lax.rem(me + k, n)},
+            device_id_type=pl.DeviceIdType.MESH,
+        )
+    pl.semaphore_wait(barrier, n - 1)
+
+    there, home = {}, {}
+    for i in list(range(near, n)) + list(range(1, near)):
+        there[i] = pltpu.make_async_remote_copy(
+            src_ref=sending.at[target(i)],
+            dst_ref=held.at[i],
+            send_sem=send_sem.at[i],
+            recv_sem=recv_sem.at[i],
+            device_id={"req": target(i)},
+            device_id_type=pl.DeviceIdType.MESH,
+        )
+        there[i].start()
+    own = pltpu.make_async_copy(sending.at[me], held.at[0], own_sem.at[0])
+    own.start()
+
+    tile = 256 if width % 256 == 0 else 128
+    model = down.shape[2]
+    wide = 512
+
+    def chunk(first, last, wait_weights):
+        count = last - first
+        for i in range(first, last):
+            if i == 0:
+                own.wait()
+            else:
+                there[i].wait_recv()
+        for j in range(slices):
+            rows_at = pl.ds(j * room, room)
+            if wait_weights:
+                weights[3 * j].wait()
+                weights[3 * j + 1].wait()
+
+            @pl.loop(0, width // tile)
+            def _(f):
+                at = pl.ds(pl.multiple_of(f * tile, tile), tile)
+                rows = held[first:last, rows_at, :].reshape(count * room, model)
+                g = jnp.dot(rows, gate[j, :, at], preferred_element_type=jnp.float32)
+                u = jnp.dot(rows, up[j, :, at], preferred_element_type=jnp.float32)
+                hidden[: count * room, at] = (g / (1.0 + jnp.exp(-g)) * u).astype(jnp.bfloat16)
+
+            if wait_weights:
+                weights[3 * j + 2].wait()
+
+            @pl.loop(0, model // wide)
+            def _(c):
+                at = pl.ds(pl.multiple_of(c * wide, wide), wide)
+                produced = jnp.dot(
+                    hidden[: count * room, :], down[j, :, at], preferred_element_type=jnp.float32
+                )
+                held[first:last, rows_at, at] = produced.astype(jnp.bfloat16).reshape(
+                    count, room, wide
+                )
+
+        for i in range(first, last):
+            if i == 0:
+                continue
+            home[i] = pltpu.make_async_remote_copy(
+                src_ref=held.at[i],
+                dst_ref=back.at[me],
+                send_sem=home_sem.at[i],
+                recv_sem=back_sem.at[i],
+                device_id={"req": source(i)},
+                device_id_type=pl.DeviceIdType.MESH,
+            )
+            home[i].start()
+
+    chunk(0, near, True)
+    own_back = pltpu.make_async_copy(held.at[0], back.at[me], own_sem.at[1])
+    own_back.start()
+    chunk(near, near + near // 2, False)
+    chunk(near + near // 2, n, False)
+    own_back.wait()
+    for i in range(1, n):
+        there[i].wait_send()
+        home[i].wait()
+    block = out_ref.shape[2]
+    returned = back[...].reshape(-1, model)
+    for b in range(out_ref.shape[0]):
+        at = pl.ds(b * block, block)
+        part = returned[:, b * block : (b + 1) * block]
+        routed = jnp.dot(high_ref[...], part, preferred_element_type=jnp.float32) + jnp.dot(
+            low_ref[...], part, preferred_element_type=jnp.float32
+        )
+        out_ref[b] = (routed + shared_ref[:, at]).astype(jnp.bfloat16)
+
+
+def run_experts(sending, gate, up, down, high, low, shared, n_blk, collective_id):
+    n, taken, model = sending.shape
+    slices, _, width = gate.shape
+    rows = shared.shape[0]
+    anywhere = pl.BlockSpec(memory_space=pl.ANY)
+    vmem = pl.BlockSpec(memory_space=pltpu.VMEM)
+    return pl.pallas_call(
+        functools.partial(experts_kernel, n),
+        out_shape=jax.ShapeDtypeStruct((n_blk, rows, model // n_blk), jnp.bfloat16),
+        in_specs=[anywhere] * 4 + [vmem] * 3,
+        out_specs=vmem,
+        scratch_shapes=[
+            pltpu.VMEM(gate.shape, gate.dtype),
+            pltpu.VMEM(up.shape, up.dtype),
+            pltpu.VMEM(down.shape, down.dtype),
+            pltpu.VMEM((n, taken, model), jnp.bfloat16),
+            pltpu.VMEM((n // 2 * taken // slices, width), jnp.bfloat16),
+            pltpu.VMEM((n, taken, model), jnp.bfloat16),
+            pltpu.SemaphoreType.DMA((3 * slices,)),
+            pltpu.SemaphoreType.DMA((n,)),
+            pltpu.SemaphoreType.DMA((n,)),
+            pltpu.SemaphoreType.DMA((n,)),
+            pltpu.SemaphoreType.DMA((n,)),
+            pltpu.SemaphoreType.DMA((2,)),
+        ],
+        compiler_params=pltpu.CompilerParams(
+            collective_id=collective_id, has_side_effects=True, vmem_limit_bytes=60 * MIB
+        ),
+        name="experts",
+    )(sending, gate, up, down, high, low, shared)
 
 
 def attention_kernel(
@@ -251,10 +408,11 @@
     inverse = inverse_of(migration)
 
     here = step_inputs.reshape(rows, width_local)
-    x_local = permute_rows(here, migration, (0, 1))
-    all_parents = lax.all_gather(parents, "req")
-    all_routes = lax.all_gather(routes, "req")
-    my_parents = lax.dynamic_index_in_dim(all_parents, migration[req_index], 0, False)
+    padded = jnp.pad(parents, ((0, 0), (0, -parents.shape[1] % HEAD_WIDTH)))
+    x_local, all_parents = permute_rows(here, migration, (0, 1), (padded,))
+    my_parents = lax.dynamic_index_in_dim(all_parents, migration[req_index], 0, False)[
+        :, : parents.shape[1]
+    ]
     x = gather_columns(x_local, "blk", 2)
     normed_x = norm_rows(x, attention_gain)
     q_local = jnp.dot(normed_x, query_weight, preferred_element_type=jnp.float32)
@@ -310,83 +468,47 @@
         x_local.astype(jnp.float32)
         + jnp.dot(heads, output_weight, preferred_element_type=jnp.float32)
     ).astype(jnp.bfloat16)
-    attended_local = permute_rows(attended_there, inverse, (6, 7))
+    (attended_local,) = permute_rows(attended_there, inverse, (6, 7))
     attended = gather_columns(attended_local, "blk", 8)
     normed_h = norm_rows(attended, feedforward_gain)
 
+    room = steps * CAP
     slice_ids = (
         jnp.arange(n_req, dtype=jnp.int32)[:, None] * n_blk + blk_index
     ) * slices_dev + jnp.arange(slices_dev, dtype=jnp.int32)[None, :]
-    targets = slice_ids // split_count
+    targets = (slice_ids // split_count).reshape(-1)
     chosen = routes.reshape(rows, TOPK)
     named = jnp.any(chosen[:, :, None] == jnp.arange(E, dtype=jnp.int32), axis=1)
+    match = jnp.any(chosen[None] == targets[:, None, None], axis=-1)
+    below = (row_ids[:, None] <= row_ids[None, :]).astype(jnp.bfloat16)
+    places = jnp.dot(
+        match.astype(jnp.bfloat16), below, preferred_element_type=jnp.float32
+    ).astype(jnp.int32)
+    places = jnp.where(match, places - 1, -1)
+    taken = places[:, None, :] == jnp.arange(room, dtype=jnp.int32)[None, :, None]
+    dispatch = taken.reshape(-1, rows)
+    sending = (
+        jnp.dot(dispatch.astype(jnp.bfloat16), normed_h, preferred_element_type=jnp.float32)
+        .astype(jnp.bfloat16)
+        .reshape(n_req, slices_dev * room, model_width)
+    )
     logits = jnp.dot(normed_h, router_weight, preferred_element_type=jnp.float32)
     raised = jnp.where(named, jnp.exp(jnp.where(named, logits, 0.0)), 0.0)
     gates = raised / jnp.sum(raised, axis=1, keepdims=True)
-    match = jnp.any(chosen[None, None] == targets[:, :, None, None], axis=-1)
-    places = jnp.cumsum(
-        match.reshape(n_req, slices_dev * rows).astype(jnp.int32), axis=1
-    ).reshape(match.shape)
-    places = jnp.where(match, places - 1, -1)
-    my_targets = targets[req_index]
-    arriving = jnp.sum(
-        jnp.any(
-            all_routes.reshape(n_req, rows, TOPK)[:, None]
-            == my_targets[None, :, None, None],
-            axis=-1,
-        ).astype(jnp.int32),
-        axis=2,
-    )
-    ends = jnp.cumsum(arriving, axis=1)
-    starts = ends - arriving
-    expert_of = (targets[:, :, None] == jnp.arange(E, dtype=jnp.int32)).astype(jnp.float32)
-    gate_of = jnp.einsum(
-        "rje,ie->rji", expert_of, gates, precision=lax.Precision.HIGHEST
-    )
-
-    def experts(room):
-        slots = jnp.arange(room, dtype=jnp.int32)
-        taken = places[:, None] == slots[None, :, None, None]
-        dispatch = jnp.any(taken, axis=2).reshape(n_req * room, rows).astype(jnp.bfloat16)
-        mixing = jnp.sum(jnp.where(taken, gate_of[:, None], 0.0), axis=2).reshape(
-            n_req * room, rows
-        )
-        sending = (
-            jnp.dot(dispatch, normed_h, preferred_element_type=jnp.float32)
-            .astype(jnp.bfloat16)
-            .reshape(n_req, room, model_width)
-        )
-        (arrived,) = push([sending], "req", 9)
-        members = arrived.reshape(n_req * room, model_width)
-        mine = (
-            (slots[None, :, None] >= starts[:, None]) & (slots[None, :, None] < ends[:, None])
-        ).reshape(n_req * room, slices_dev)
-        produced = jnp.zeros((n_req * room, model_width), jnp.float32)
-        for j in range(slices_dev):
-            gate_part = jnp.dot(members, expert_gate[j], preferred_element_type=jnp.float32)
-            up_part = jnp.dot(members, expert_up[j], preferred_element_type=jnp.float32)
-            hidden = jnp.where(
-                mine[:, j : j + 1], jax.nn.silu(gate_part) * up_part, 0.0
-            ).astype(jnp.bfloat16)
-            produced += jnp.dot(hidden, expert_down[j], preferred_element_type=jnp.float32)
-        (returned,) = push(
-            [produced.astype(jnp.bfloat16).reshape(n_req, room, model_width)], "req", 10
-        )
-        returned = returned.reshape(n_req * room, model_width)
-        high = mixing.astype(jnp.bfloat16)
-        low = (mixing - high.astype(jnp.float32)).astype(jnp.bfloat16)
-        return jnp.dot(high.T, returned, preferred_element_type=jnp.float32) + jnp.dot(
-            low.T, returned, preferred_element_type=jnp.float32
-        )
-
-    routed = experts(slices_dev * steps * CAP)
+    expert_of = (targets[:, None] == jnp.arange(E, dtype=jnp.int32)).astype(jnp.float32)
+    gate_of = jnp.dot(gates, expert_of.T, precision=lax.Precision.HIGHEST)
+    mixing = jnp.where(
+        jnp.transpose(taken, (2, 0, 1)), gate_of[:, :, None], 0.0
+    ).reshape(rows, -1)
+    high = mixing.astype(jnp.bfloat16)
+    low = (mixing - high.astype(jnp.float32)).astype(jnp.bfloat16)
     shared_act = (
         jax.nn.silu(jnp.dot(normed_h, shared_gate, preferred_element_type=jnp.float32))
         * jnp.dot(normed_h, shared_up, preferred_element_type=jnp.float32)
     ).astype(jnp.bfloat16)
-    terms = routed + jnp.dot(shared_act, shared_down, preferred_element_type=jnp.float32)
-    blocks = jnp.transpose(
-        terms.astype(jnp.bfloat16).reshape(rows, n_blk, width_local), (1, 0, 2)
+    shared = jnp.dot(shared_act, shared_down, preferred_element_type=jnp.float32)
+    blocks = run_experts(
+        sending, expert_gate, expert_up, expert_down, high, low, shared, n_blk, 9
     )
     (blocks,) = push([blocks], "blk", 11)
     summed = jnp.sum(blocks.astype(jnp.float32), axis=0)

time: 398 us -> 299 us (0.75)
  matrix products: 73.5 us -> 17.8 us
  blocking collectives: 36.9 us -> 0 us
    pallas_call x12 -> x10, Pallas kernels: 223 us -> 97.7 us  [push(): pl.pallas_call(functools.partial(push_kernel, axis, n, count, gather), ou...]
    pallas_call x0 -> x1, Pallas kernels: none -> 122 us  [run_experts(): pl.pallas_call(functools.partial(experts_kernel, n), out_shape=jax.ShapeD...]
    dot_general x8 -> x3, matrix products: 57.9 us -> 2.68 us  [the longest x1 2.36 us: per_device(): jnp.dot(dispatch.astype(jnp.bfloat16), normed_h, preferred_element_type=j...]
    all_gather x2 -> x0, blocking collectives: 36.9 us -> none  [the longest x1 22.2 us: per_device(): all_routes = lax.all_gather(routes, 'req')]
where the time goes in v2:
time: 299 us; the launch traced here: 298 us
  Pallas kernels  232 us (78%)
  local copies, waits for them, and re-layouts  25.3 us (8%)
  other arithmetic  21.3 us (7%)
  matrix products  17.8 us (6%)
    pallas_call x1, Pallas kernels, run_experts(): pl.pallas_call(functools.partial(experts_kernel, n), out_shape=jax.ShapeD...  122 us
    pallas_call x10, Pallas kernels, push(): pl.pallas_call(functools.partial(push_kernel, axis, n, count, gather), ou...  97.7 us
    pallas_call x1, Pallas kernels, attention_part(): pl.pallas_call(attention_kernel, out_shape=[jax.ShapeDtypeStruct(q.shape,...  11 us
    unnamed x41, local copies, waits for them, and re-layouts  7.16 us
    dot_general x1, matrix products, per_device(): jnp.dot(shared_act, shared_down, preferred_element_type=jnp.float32)  6.13 us

profile of v2, /device:TPU:9, one launch (start us, length us, event | category | flops | bytes accessed | tf_op | source)
XLA Modules:
  0.0 298.3 jit_solution(16921640042800965352)
XLA Ops:
  0.0 1.4 dynamic_slice.15
  3.3 1.2 dynamic_slice.14
  4.6 0.7 pad_add_fusion.tail_ref
  5.3 0.7 dynamic-slice_bitcast_fusion
  6.1 0.8 select_reduce_fusion.1
  6.9 1.2 fusion.34
  8.0 1.2 pad.5.refs_1_
  9.3 0.5 multiply_power_fusion
  9.8 1.3 compare_and_fusion
  11.0 0.7 compare_select_fusion.1
  11.9 0.8 eq.135
  12.8 0.6 pad_clamp_fusion.1
  13.7 0.7 mul.132
  14.4 8.4 %push_req_0.1 = (bf16[8,16,640]{2,1,0:T(8,128)(2,1)}, s32[8,1,128]{2,1,0:T(1,128)}) custom-call(bf16[8,16,640]{2,1,0:T(8,128)(2,1)} %bitcast.96, s32[1,128]{1,0:T(1,128)} %pad.5.refs_1_), custom_call_target="tpu_custom_call" | custom-call | tf_op jit(solution)/shard_map/push_req_0/pallas_call | solution.py:75
  22.8 1.6 gather_fusion
  24.4 1.4 broadcast_select_fusion.1.refs_0_
  25.9 5.5 %push_req_1.1 = bf16[8,16,640]{2,1,0:T(8,128)(2,1)} custom-call(bf16[8,16,640]{2,1,0:T(8,128)(2,1)} %broadcast_select_fusion.1.refs_0_), custom_call_target="tpu_custom_call" | custom-call | tf_op jit(solution)/shard_map/push_req_1/pallas_call | solution.py:75
  31.4 0.6 dynamic-slice_bitcast_fusion.1
  32.2 0.9 fusion.28
  33.2 0.7 eq.144
  33.9 1.8 copy.39
  35.7 13.0 %push_blk_2.1 = bf16[4,128,640]{2,1,0:T(8,128)(2,1)} custom-call(bf16[128,640]{1,0:T(8,128)(2,1)} %bitcast.85), custom_call_target="tpu_custom_call" | custom-call | tf_op jit(solution)/shard_map/push_blk_2/pallas_call | solution.py:75
  48.7 1.3 fusion
  50.0 2.3 convert_bitcast_fusion.1
  52.3 2.8 copy.35
  55.1 1.8 fusion.7
  56.9 1.0 convolution_convert_fusion.2.refs_1_
  58.0 1.4 convolution_convert_fusion.1.refs_0_
  59.4 12.8 %push_blk_3.1 = (bf16[4,128,640]{2,1,0:T(8,128)(2,1)}, bf16[4,128,256]{2,1,0:T(8,128)(2,1)}) custom-call(bf16[128,640]{1,0:T(8,128)(2,1)} %convolution_convert_fusion.1.refs_0_, bf16[128,256]{1,0:T(8,128)(2,1)} %convolution_convert_fusion.2.refs_1_), custom_call_target="tpu_custom_call" | custom-call | tf_op jit(solution)/shard_map/push_blk_3/pallas_call | solution.py:75
  72.1 1.2 copy.42
  73.4 1.9 copy-done.2
  75.3 11.0 %attention_part.1 = (bf16[128,2560]{1,0:T(8,128)(2,1)S(1)}, f32[128,128]{1,0:T(8,128)S(1)}) custom-call(s32[2]{0:T(128)S(1)} %pad_add_fusion.tail_ref, bf16[128,2560]{1,0:T(8,128)(2,1)S(1)} %bitcast.77, bf16[128,1024]{1,0:T(8,128)(2,1)S(1)} %bitcast.78, bf16[128,128]{1,0:T(8,128)(2,1)S(1)} %fusion.25.parent_ref, f32[128,128]{1,0:T(8,128)S(1)} %get-tuple-element.31.cos_ref, ...), custom_call_target="tpu_custom_call" | custom-call | tf_op jit(solution)/shard_map/attention_part/pallas_call | solution.py:322
  86.3 0.8 copy-done.3
  87.1 0.6 copy-done.7
  87.8 10.6 %push_blk_4.1 = (bf16[4,32,2560]{2,1,0:T(8,128)(2,1)}, f32[4,32,128]{2,1,0:T(8,128)}) custom-call(bf16[4,32,2560]{2,1,0:T(8,128)(2,1)} %bitcast.79, f32[4,32,128]{2,1,0:T(8,128)} %bitcast.80), custom_call_target="tpu_custom_call" | custom-call | tf_op jit(solution)/shard_map/push_blk_4/pallas_call | solution.py:75
  98.4 1.1 copy-done.4
  99.5 0.8 copy-done.6
  100.4 0.5 merge.1.refs_0_
  100.8 0.7 copy-done.5
  101.5 9.9 %push_blk_5.1 = bf16[4,32,2560]{2,1,0:T(8,128)(2,1)} custom-call(bf16[32,2560]{1,0:T(8,128)(2,1)} %copy-done.5), custom_call_target="tpu_custom_call" | custom-call | tf_op jit(solution)/shard_map/push_blk_5/pallas_call | solution.py:75
  111.4 3.5 %fusion.9 = bf16[128,640]{1,0:T(8,128)(2,1)} fusion(bf16[128,2560]{1,0:T(8,128)(2,1)} %bitcast.84, bf16[2560,640]{1,0:T(8,128)(2,1)} %param.25, bf16[128,640]{1,0:T(8,128)(2,1)S(1)} %bitcast.86), kind=kOutput, calls=%fused_computation.22 | convolution fusion | flops 419676160 | bytes 4259840 | tf_op jit(solution)/shard_map/dot_general | solution.py:469
  114.9 8.6 %push_req_6.1 = bf16[8,16,640]{2,1,0:T(8,128)(2,1)} custom-call(bf16[8,16,640]{2,1,0:T(8,128)(2,1)} %bitcast.92), custom_call_target="tpu_custom_call" | custom-call | tf_op jit(solution)/shard_map/push_req_6/pallas_call | solution.py:75
  123.5 1.5 gather_fusion.1
  125.0 0.8 broadcast_select_fusion.refs_0_
  125.8 8.4 %push_req_7.1 = bf16[8,16,640]{2,1,0:T(8,128)(2,1)} custom-call(bf16[8,16,640]{2,1,0:T(8,128)(2,1)} %broadcast_select_fusion.refs_0_), custom_call_target="tpu_custom_call" | custom-call | tf_op jit(solution)/shard_map/push_req_7/pallas_call | solution.py:75
  134.1 10.4 %push_blk_8.1 = bf16[4,128,640]{2,1,0:T(8,128)(2,1)} custom-call(bf16[128,640]{1,0:T(8,128)(2,1)} %bitcast.87), custom_call_target="tpu_custom_call" | custom-call | tf_op jit(solution)/shard_map/push_blk_8/pallas_call | solution.py:75
  144.6 1.3 fusion.1
  145.9 1.4 fusion.15
  147.3 1.1 copy.38
  148.5 0.4 copy.40
  148.9 0.3 copy-done.16
  149.2 0.4 fusion.5
  149.6 0.6 copy-done.14
  150.1 0.3 fusion.36
  150.8 0.3 copy-done.10
  151.1 0.7 subtract_convert_fusion.low_ref
  151.8 0.7 fusion.24.high_ref
  152.5 2.8 fusion.37
  155.3 6.1 %fusion.14.shared_ref = f32[128,2560]{1,0:T(8,128)} fusion(bf16[768,2560]{1,0:T(8,128)(2,1)} %param.39, bf16[128,2560]{0,1:T(8,128)(2,1)S(1)} %fusion.5, bf16[2560,768]{1,0:T(8,128)(2,1)} %param.38, f32[128,768]{1,0:T(8,128)S(1)} %fusion.37), kind=kOutput, calls=%fused_computation.31 | convolution fusion | flops 1007222784 | bytes 10223616 | tf_op jit(solution)/shard_map/dot_general | solution.py:509
  161.4 2.4 convolution_convert_fusion
  163.8 122.4 %experts.1.refs_0_ = bf16[4,128,640]{2,1,0:T(8,128)(2,1)} custom-call(bf16[8,64,2560]{2,1,0:T(8,128)(2,1)} %bitcast.82, bf16[2,2560,1536]{2,1,0:T(8,128)(2,1)} %gate_hbm.1, bf16[2,2560,1536]{2,1,0:T(8,128)(2,1)} %up_hbm.1, bf16[2,1536,2560]{2,1,0:T(8,128)(2,1)} %down_hbm.1, bf16[128,512]{1,0:T(8,128)(2,1)} %fusion.24.high_ref, ...), custom_call_target="tpu_custom_call" | custom-call | tf_op jit(solution)/shard_map/experts/pallas_call | solution.py:231
  286.2 10.2 %push_blk_11.1 = bf16[4,128,640]{2,1,0:T(8,128)(2,1)} custom-call(bf16[4,128,640]{2,1,0:T(8,128)(2,1)} %experts.1.refs_0_), custom_call_target="tpu_custom_call" | custom-call | tf_op jit(solution)/shard_map/push_blk_11/pallas_call | solution.py:75
  296.4 1.2 convert_reduce_fusion
  297.6 0.7 fusion.21
  (56 shorter events, 1.5 us)
Async XLA Ops:
  0.0 58.0 %copy-start = (bf16[2560,640]{1,0:T(8,128)(2,1)S(1)}, bf16[2560,640]{1,0:T(8,128)(2,1)}, u32[]{:S(2)}) copy-start(bf16[2560,640]{1,0:T(8,128)(2,1)} %param.23) | copy-start | bytes 9830404
  11.9 0.9 copy-start.18
  55.1 1.8 copy-start.13
  72.1 1.2 copy-start.15
  73.4 1.9 copy-start.2
  86.3 0.8 copy-start.3
  87.1 0.6 copy-start.7
  87.8 23.6 %copy-start.11 = (bf16[8,16,640]{2,1,0:T(8,128)(2,1)S(1)}, bf16[8,16,640]{2,1,0:T(8,128)(2,1)}, u32[]{:S(2)}) copy-start(bf16[8,16,640]{2,1,0:T(8,128)(2,1)} %push_req_1.1) | copy-start | bytes 491524
  98.4 1.1 copy-start.4
  99.5 0.8 copy-start.6
  100.8 0.7 copy-start.5
  111.4 13.6 %copy-start.17 = (pred[8]{0:T(512)(128)(4,1)S(1)}, pred[8]{0:T(512)(128)(4,1)}, u32[]{:S(2)}) copy-start(pred[8]{0:T(512)(128)(4,1)} %get-tuple-element.29) | copy-start | bytes 28
  145.9 2.5 copy-start.8
  148.4 0.7 copy-start.16
  149.2 1.0 copy-start.14
  149.2 1.2 copy-start.19
  150.1 0.9 copy-start.10
  155.3 6.1 %copy-start.9 = (bf16[128,4,640]{0,2,1:T(8,128)(2,1)S(1)}, bf16[128,4,640]{0,2,1:T(8,128)(2,1)}, u32[]{:S(2)}) copy-start(bf16[128,4,640]{0,2,1:T(8,128)(2,1)} %copy.38) | copy-start | bytes 1966084
  163.8 134.5 %copy-start.1 = (bf16[2560,640]{1,0:T(8,128)(2,1)S(1)}, bf16[2560,640]{1,0:T(8,128)(2,1)}, u32[]{:S(2)}) copy-start(bf16[2560,640]{1,0:T(8,128)(2,1)} %param.23) | copy-start | bytes 9830404
  286.2 11.4 %copy-start.12 = (bf16[8,16,640]{2,1,0:T(8,128)(2,1)S(1)}, bf16[8,16,640]{2,1,0:T(8,128)(2,1)}, u32[]{:S(2)}) copy-start(bf16[8,16,640]{2,1,0:T(8,128)(2,1)} %push_req_7.1) | copy-start | bytes 491524

commit v3 on v2

--- a/solution.py
+++ b/solution.py
@@ -87,24 +87,115 @@
     )(*arrays)
 
 
-def gather_columns(array, axis, collective_id):
-    (blocks,) = push([array], axis, collective_id, gather=True)
-    return jnp.transpose(blocks, (1, 0, 2)).reshape(array.shape[0], -1)
-
-
-def permute_rows(rows, block_for, ids, beside=()):
-    n = lax.axis_size("req")
-    pieces = rows.reshape(n, rows.shape[0] // n, rows.shape[1])
-    spread, *gathered = push(
-        [pieces, *beside], "req", ids[0], gather=(False,) + (True,) * len(beside)
-    )
-    (arrived,) = push([jnp.take(spread, block_for, axis=0)], "req", ids[1])
-    return (arrived.reshape(rows.shape), *gathered)
+def route_kernel(n, n_blk, extra, block_for, gain_ref, pieces, *refs):
+    besides, refs = refs[:extra], refs[extra:]
+    normed_ref, rows_ref, *refs = refs
+    gathered, refs = refs[:extra], refs[extra:]
+    spread, staged, landed, wide, hop_send, hop_recv, local_sem = refs
+    me, blk = lax.axis_index("req"), lax.axis_index("blk")
+    barrier = pltpu.get_barrier_semaphore()
+
+    def at(axis, k):
+        here, size = (me, n) if axis == "req" else (blk, n_blk)
+        return {axis: lax.rem(here + k, size)}
+
+    partners = [("req", k) for k in range(1, n)] + [("blk", k) for k in range(1, n_blk)]
+    for axis, k in partners:
+        pl.semaphore_signal(
+            barrier, inc=1, device_id=at(axis, k), device_id_type=pl.DeviceIdType.MESH
+        )
+    pl.semaphore_wait(barrier, len(partners))
+
+    def send(source, landing, phase, axis, k):
+        copy = pltpu.make_async_remote_copy(
+            src_ref=source,
+            dst_ref=landing,
+            send_sem=hop_send.at[phase, k],
+            recv_sem=hop_recv.at[phase, k],
+            device_id=at(axis, k),
+            device_id_type=pl.DeviceIdType.MESH,
+        )
+        copy.start()
+        return copy
+
+    def keep(source, landing, number):
+        copy = pltpu.make_async_copy(source, landing, local_sem.at[number])
+        copy.start()
+        return copy
+
+    copies = [
+        send(pieces.at[lax.rem(me + k, n)], spread.at[me], 0, "req", k) for k in range(1, n)
+    ]
+    copies.append(keep(pieces.at[me], spread.at[me], 0))
+    late = []
+    for i in range(extra):
+        late += [send(besides[i], gathered[i].at[me], 3 + i, "req", k) for k in range(1, n)]
+        late.append(keep(besides[i], gathered[i].at[me], 3 + i))
+    for copy in copies:
+        copy.wait()
+    for d in range(n):
+        staged[d] = spread[block_for[d]]
+    copies = [
+        send(staged.at[lax.rem(me + k, n)], landed.at[me], 1, "req", k) for k in range(1, n)
+    ]
+    copies.append(keep(staged.at[me], landed.at[me], 1))
+    for copy in copies:
+        copy.wait()
+    copies = [send(landed, wide.at[blk], 2, "blk", k) for k in range(1, n_blk)]
+    copies.append(keep(landed, wide.at[blk], 2))
+    rows_ref[...] = landed[...]
+    for copy in copies + late:
+        copy.wait()
+    rows, model = normed_ref.shape
+    width = model // n_blk
+    blocks = [wide[b].astype(jnp.float32).reshape(rows, width) for b in range(n_blk)]
+    squares = jnp.sum(blocks[0] * blocks[0], axis=1, keepdims=True)
+    for block in blocks[1:]:
+        squares += jnp.sum(block * block, axis=1, keepdims=True)
+    inverse = lax.rsqrt(squares / model + epsilon)
+    for b in range(n_blk):
+        columns = slice(b * width, (b + 1) * width)
+        normed_ref[:, columns] = (blocks[b] * inverse * gain_ref[:, columns]).astype(jnp.bfloat16)
+
+
+def route_rows(rows, block_for, gain, collective_id, beside=()):
+    n, n_blk = lax.axis_size("req"), lax.axis_size("blk")
+    count, width = rows.shape
+    extra = len(beside)
+    pieces = rows.reshape(n, count // n, width)
+    anywhere = pl.BlockSpec(memory_space=pl.ANY)
+    vmem = pl.BlockSpec(memory_space=pltpu.VMEM)
+    phases = 3 + extra
+    hops = max(n, n_blk)
+    normed, arrived, *gathered = pl.pallas_call(
+        functools.partial(route_kernel, n, n_blk, extra),
+        out_shape=[
+            jax.ShapeDtypeStruct((count, width * n_blk), jnp.bfloat16),
+            jax.ShapeDtypeStruct(pieces.shape, rows.dtype),
+        ]
+        + [jax.ShapeDtypeStruct((n,) + a.shape, a.dtype) for a in beside],
+        in_specs=[pl.BlockSpec(memory_space=pltpu.SMEM), vmem, vmem] + [anywhere] * extra,
+        out_specs=[vmem] * 2 + [anywhere] * extra,
+        scratch_shapes=[pltpu.VMEM(pieces.shape, rows.dtype)] * 3
+        + [
+            pltpu.VMEM((n_blk,) + pieces.shape, rows.dtype),
+            pltpu.SemaphoreType.DMA((phases, hops)),
+            pltpu.SemaphoreType.DMA((phases, hops)),
+            pltpu.SemaphoreType.DMA((phases,)),
+        ],
+        compiler_params=pltpu.CompilerParams(
+            collective_id=collective_id, has_side_effects=True, vmem_limit_bytes=32 * MIB
+        ),
+        name=f"route_{collective_id}",
+    )(block_for, gain.reshape(1, -1), pieces, *beside)
+    return (normed, arrived.reshape(rows.shape), *gathered)
 
 
 def experts_kernel(
-    n, sending, gate_hbm, up_hbm, down_hbm, high_ref, low_ref, shared_ref, out_ref,
-    gate, up, down, held, hidden, back, weight_sem, send_sem, recv_sem, home_sem, back_sem, own_sem,
+    n, sending, gate_hbm, up_hbm, down_hbm, shared_gate, shared_up, shared_down,
+    high_ref, low_ref, normed_ref, out_ref,
+    gate, up, down, held, hidden, back, shared_act, shared_ref,
+    weight_sem, send_sem, recv_sem, home_sem, back_sem, own_sem, *apart,
 ):
     me = lax.axis_index("req")
     near = n // 2
@@ -120,12 +211,24 @@
 
     slices, _, width = gate.shape
     room = held.shape[1] // slices
-    weights = []
-    for j in range(slices):
-        for number, (hbm, vmem) in enumerate(((gate_hbm, gate), (up_hbm, up), (down_hbm, down))):
-            copy = pltpu.make_async_copy(hbm.at[j], vmem.at[j], weight_sem.at[3 * j + number])
-            copy.start()
-            weights.append(copy)
+    last = slices - 1
+    shared_width = shared_gate.shape[1]
+    if apart:
+        places = apart
+    else:
+        columns = pl.ds(0, shared_width)
+        places = (gate.at[last, :, columns], up.at[last, :, columns], down.at[last, columns, :])
+    shared_copies = [
+        pltpu.make_async_copy(hbm, vmem, weight_sem.at[3 * slices + number])
+        for number, (hbm, vmem) in enumerate(zip((shared_gate, shared_up, shared_down), places))
+    ]
+    weights = [
+        pltpu.make_async_copy(hbm.at[j], vmem.at[j], weight_sem.at[3 * j + number])
+        for j in range(slices)
+        for number, (hbm, vmem) in enumerate(((gate_hbm, gate), (up_hbm, up), (down_hbm, down)))
+    ]
+    for copy in shared_copies + weights[: 3 * last]:
+        copy.start()
 
     barrier = pltpu.get_barrier_semaphore()
     for k in range(1, n):
@@ -154,6 +257,22 @@
     tile = 256 if width % 256 == 0 else 128
     model = down.shape[2]
     wide = 512
+
+    for copy in shared_copies:
+        copy.wait()
+    step = 256 if shared_width % 256 == 0 else shared_width
+    for f in range(0, shared_width, step):
+        at = slice(f, f + step)
+        g = jnp.dot(normed_ref[...], places[0][:, at], preferred_element_type=jnp.float32)
+        u = jnp.dot(normed_ref[...], places[1][:, at], preferred_element_type=jnp.float32)
+        shared_act[:, at] = (g / (1.0 + jnp.exp(-g)) * u).astype(jnp.bfloat16)
+    for c in range(0, model, wide):
+        at = slice(c, c + wide)
+        shared_ref[:, at] = jnp.dot(
+            shared_act[...], places[2][:, at], preferred_element_type=jnp.float32
+        )
+    for copy in weights[3 * last :]:
+        copy.start()
 
     def chunk(first, last, wait_weights):
         count = last - first
@@ -222,16 +341,20 @@
         out_ref[b] = (routed + shared_ref[:, at]).astype(jnp.bfloat16)
 
 
-def run_experts(sending, gate, up, down, high, low, shared, n_blk, collective_id):
+def run_experts(sending, experts, shared, high, low, normed, n_blk, collective_id):
     n, taken, model = sending.shape
+    gate, up, down = experts
     slices, _, width = gate.shape
-    rows = shared.shape[0]
+    rows = normed.shape[0]
+    shared_width = shared[0].shape[1]
+    fits = shared_width % HEAD_WIDTH == 0 and shared_width <= width
+    apart = [] if fits else [pltpu.VMEM(a.shape, a.dtype) for a in shared]
     anywhere = pl.BlockSpec(memory_space=pl.ANY)
     vmem = pl.BlockSpec(memory_space=pltpu.VMEM)
     return pl.pallas_call(
         functools.partial(experts_kernel, n),
         out_shape=jax.ShapeDtypeStruct((n_blk, rows, model // n_blk), jnp.bfloat16),
-        in_specs=[anywhere] * 4 + [vmem] * 3,
+        in_specs=[anywhere] * 7 + [vmem] * 3,
         out_specs=vmem,
         scratch_shapes=[
             pltpu.VMEM(gate.shape, gate.dtype),
@@ -240,18 +363,21 @@
             pltpu.VMEM((n, taken, model), jnp.bfloat16),
             pltpu.VMEM((n // 2 * taken // slices, width), jnp.bfloat16),
             pltpu.VMEM((n, taken, model), jnp.bfloat16),
-            pltpu.SemaphoreType.DMA((3 * slices,)),
+            pltpu.VMEM((rows, shared_width), jnp.bfloat16),
+            pltpu.VMEM((rows, model), jnp.float32),
+            pltpu.SemaphoreType.DMA((3 * slices + 3,)),
             pltpu.SemaphoreType.DMA((n,)),
             pltpu.SemaphoreType.DMA((n,)),
             pltpu.SemaphoreType.DMA((n,)),
             pltpu.SemaphoreType.DMA((n,)),
             pltpu.SemaphoreType.DMA((2,)),
+            *apart,
         ],
         compiler_params=pltpu.CompilerParams(
             collective_id=collective_id, has_side_effects=True, vmem_limit_bytes=60 * MIB
         ),
         name="experts",
-    )(sending, gate, up, down, high, low, shared)
+    )(sending, *experts, *shared, high, low, normed)
 
 
 def attention_kernel(
@@ -362,12 +488,6 @@
     )(parts, lse)
 
 
-def norm_rows(values, gain):
-    as_float = values.astype(jnp.float32)
-    inverse = lax.rsqrt(jnp.mean(as_float * as_float, axis=-1, keepdims=True) + epsilon)
-    return (as_float * inverse * gain).astype(jnp.bfloat16)
-
-
 def inverse_of(migration):
     slot_ids = jnp.arange(migration.shape[0], dtype=jnp.int32)
     return jnp.sum(jnp.where(migration[None, :] == slot_ids[:, None], slot_ids[None, :], 0), axis=1)
@@ -409,12 +529,10 @@
 
     here = step_inputs.reshape(rows, width_local)
     padded = jnp.pad(parents, ((0, 0), (0, -parents.shape[1] % HEAD_WIDTH)))
-    x_local, all_parents = permute_rows(here, migration, (0, 1), (padded,))
+    normed_x, x_local, all_parents = route_rows(here, migration, attention_gain, 0, (padded,))
     my_parents = lax.dynamic_index_in_dim(all_parents, migration[req_index], 0, False)[
         :, : parents.shape[1]
     ]
-    x = gather_columns(x_local, "blk", 2)
-    normed_x = norm_rows(x, attention_gain)
     q_local = jnp.dot(normed_x, query_weight, preferred_element_type=jnp.float32)
     kv_local = jnp.dot(normed_x, key_value_weight, preferred_element_type=jnp.float32)
     q_blocks, kv_blocks = push(
@@ -468,9 +586,7 @@
         x_local.astype(jnp.float32)
         + jnp.dot(heads, output_weight, preferred_element_type=jnp.float32)
     ).astype(jnp.bfloat16)
-    (attended_local,) = permute_rows(attended_there, inverse, (6, 7))
-    attended = gather_columns(attended_local, "blk", 8)
-    normed_h = norm_rows(attended, feedforward_gain)
+    normed_h, attended_local = route_rows(attended_there, inverse, feedforward_gain, 6)
 
     room = steps * CAP
     slice_ids = (
@@ -502,13 +618,15 @@
     ).reshape(rows, -1)
     high = mixing.astype(jnp.bfloat16)
     low = (mixing - high.astype(jnp.float32)).astype(jnp.bfloat16)
-    shared_act = (
-        jax.nn.silu(jnp.dot(normed_h, shared_gate, preferred_element_type=jnp.float32))
-        * jnp.dot(normed_h, shared_up, preferred_element_type=jnp.float32)
-    ).astype(jnp.bfloat16)
-    shared = jnp.dot(shared_act, shared_down, preferred_element_type=jnp.float32)
     blocks = run_experts(
-        sending, expert_gate, expert_up, expert_down, high, low, shared, n_blk, 9
+        sending,
+        (expert_gate, expert_up, expert_down),
+        (shared_gate, shared_up, shared_down),
+        high,
+        low,
+        normed_h,
+        n_blk,
+        9,
     )
     (blocks,) = push([blocks], "blk", 11)
     summed = jnp.sum(blocks.astype(jnp.float32), axis=0)

time: 299 us -> 259 us (0.87)
  other arithmetic: 21.3 us -> 6.48 us
  Pallas kernels: 232 us -> 221 us
  matrix products: 17.8 us -> 9.5 us
  local copies, waits for them, and re-layouts: 25.3 us -> 19.4 us
    pallas_call x10 -> x4, Pallas kernels: 97.7 us -> 43.4 us  [push(): pl.pallas_call(functools.partial(push_kernel, axis, n, count, gather), ou...]
    pallas_call x0 -> x2, Pallas kernels: none -> 43.6 us  [route_rows(): pl.pallas_call(functools.partial(route_kernel, n, n_blk, extra), out_shap...]
    dot_general x2 -> x0, matrix products: 8.97 us -> none  [the longest x1 6.13 us: per_device(): jnp.dot(shared_act, shared_down, preferred_element_type=jnp.float32)]
    convert_element_type x4 -> x0, other arithmetic: 4.57 us -> none  [the longest x2 2.34 us: norm_rows(): as_float = values.astype(jnp.float32)]
    convert_element_type x2 -> x0, local copies, waits for them, and re-layouts: 3.18 us -> none  [norm_rows(): as_float = values.astype(jnp.float32)]
    gather x2 -> x0, local copies, waits for them, and re-layouts: 3.11 us -> none  [permute_rows(): arrived, = push([jnp.take(spread, block_for, axis=0)], 'req', ids[1])]
    unnamed x41 -> x31, local copies, waits for them, and re-layouts: 7.16 us -> 8.18 us
where the time goes in v3:
time: 259 us; the launch traced here: 258 us
  Pallas kernels  221 us (85%)
  local copies, waits for them, and re-layouts  19.4 us (7%)
  matrix products  9.5 us (4%)
  other arithmetic  6.48 us (3%)
    pallas_call x1, Pallas kernels, run_experts(): pl.pallas_call(functools.partial(experts_kernel, n), out_shape=jax.ShapeD...  122 us
    pallas_call x2, Pallas kernels, route_rows(): pl.pallas_call(functools.partial(route_kernel, n, n_blk, extra), out_shap...  43.6 us
    pallas_call x4, Pallas kernels, push(): pl.pallas_call(functools.partial(push_kernel, axis, n, count, gather), ou...  43.4 us
    pallas_call x1, Pallas kernels, attention_part(): pl.pallas_call(attention_kernel, out_shape=[jax.ShapeDtypeStruct(q.shape,...  10.9 us
    unnamed x31, local copies, waits for them, and re-layouts  8.18 us

profile of v3, /device:TPU:9, one launch (start us, length us, event | category | flops | bytes accessed | tf_op | source)
XLA Modules:
  0.0 258.3 jit_solution(4074113995273562982)
XLA Ops:
  0.0 0.0 copy-start
  0.0 1.4 dynamic_slice.15
  3.3 1.2 dynamic_slice.14
  4.6 0.7 pad_add_fusion.tail_ref
  5.3 0.7 dynamic-slice_bitcast_fusion
  6.0 0.1 select_reduce_fusion
  6.1 0.7 fusion.17
  6.7 0.7 pad.5.refs_0_
  7.4 0.8 select_reduce_fusion.1.block_for
  8.2 0.1 iota_add_fusion
  8.3 0.1 add.131
  8.3 0.8 eq.132
  9.1 0.1 compare_reduce_fusion
  9.2 0.1 fusion.4
  9.4 0.1 add_bitcast_fusion
  9.5 0.1 eq.140
  9.5 0.7 reshape.140.gain_ref
  10.3 0.7 reshape.139.gain_ref
  11.0 0.1 bitcast_compare_fusion
  11.1 0.3 fusion.11
  11.4 0.1 pad_maximum_fusion
  11.5 0.7 eq.143
  12.3 1.8 copy.34
  14.0 0.9 copy-done.9
  15.0 0.7 copy-done.12
  15.6 22.3 %route_0.1 = (bf16[128,2560]{1,0:T(8,128)(2,1)S(1)}, bf16[8,16,640]{2,1,0:T(8,128)(2,1)S(1)}, s32[8,1,128]{2,1,0:T(1,128)S(1)}) custom-call(s32[8]{0:T(128)S(1)} %copy-done.12, f32[1,2560]{1,0:T(1,128)S(1)} %reshape.140.gain_ref, bf16[8,16,640]{2,1,0:T(8,128)(2,1)S(1)} %bitcast.60, s32[1,128]{1,0:T(1,128)S(1)} %pad.5.refs_0_), custom_call_target="tpu_custom_call" | custom-call | tf_op jit(solution)/shard_map/route_0/pallas_call | solution.py:170
  37.9 0.0 copy-start.7
  37.9 0.7 copy-done.7
  38.6 0.1 concatenate.9
  38.7 0.1 fusion.8.parent_ref
  38.8 2.3 convolution_convert_fusion.2.refs_1_
  41.0 0.0 copy-done
  41.0 1.3 convolution_convert_fusion.1.refs_0_
  42.4 12.8 %push_blk_3.1 = (bf16[4,128,640]{2,1,0:T(8,128)(2,1)}, bf16[4,128,256]{2,1,0:T(8,128)(2,1)}) custom-call(bf16[128,640]{1,0:T(8,128)(2,1)} %convolution_convert_fusion.1.refs_0_, bf16[128,256]{1,0:T(8,128)(2,1)} %convolution_convert_fusion.2.refs_1_), custom_call_target="tpu_custom_call" | custom-call | tf_op jit(solution)/shard_map/push_blk_3/pallas_call | solution.py:75
  55.2 1.1 copy.36
  56.3 1.0 copy.37
  57.3 0.0 copy-start.3
  57.3 1.9 copy-done.3
  59.2 10.9 %attention_part.1 = (bf16[128,2560]{1,0:T(8,128)(2,1)S(1)}, f32[128,128]{1,0:T(8,128)S(1)}) custom-call(s32[2]{0:T(128)S(1)} %pad_add_fusion.tail_ref, bf16[128,2560]{1,0:T(8,128)(2,1)S(1)} %bitcast.54, bf16[128,1024]{1,0:T(8,128)(2,1)S(1)} %bitcast.55, bf16[128,128]{1,0:T(8,128)(2,1)S(1)} %fusion.8.parent_ref, f32[128,128]{1,0:T(8,128)S(1)} %get-tuple-element.32.cos_ref, ...), custom_call_target="tpu_custom_call" | custom-call | tf_op jit(solution)/shard_map/attention_part/pallas_call | solution.py:448
  70.0 0.0 copy-start.4
  70.1 0.8 copy-done.4
  70.9 0.6 copy-done.11
  71.5 10.6 %push_blk_4.1 = (bf16[4,32,2560]{2,1,0:T(8,128)(2,1)}, f32[4,32,128]{2,1,0:T(8,128)}) custom-call(bf16[4,32,2560]{2,1,0:T(8,128)(2,1)} %bitcast.57, f32[4,32,128]{2,1,0:T(8,128)} %bitcast.61), custom_call_target="tpu_custom_call" | custom-call | tf_op jit(solution)/shard_map/push_blk_4/pallas_call | solution.py:75
  82.2 1.1 copy-done.5
  83.3 0.8 copy-done.10
  84.1 0.5 merge.1.refs_0_
  84.6 0.0 copy-start.6
  84.6 0.7 copy-done.6
  85.2 9.9 %push_blk_5.1 = bf16[4,32,2560]{2,1,0:T(8,128)(2,1)} custom-call(bf16[32,2560]{1,0:T(8,128)(2,1)} %copy-done.6), custom_call_target="tpu_custom_call" | custom-call | tf_op jit(solution)/shard_map/push_blk_5/pallas_call | solution.py:75
  95.1 0.0 copy-start.13
  95.1 0.0 copy-done.8
  95.1 2.8 %fusion = bf16[128,640]{1,0:T(8,128)(2,1)S(1)} fusion(bf16[128,2560]{1,0:T(8,128)(2,1)} %bitcast.64, bf16[2560,640]{1,0:T(8,128)(2,1)} %param.23, bf16[128,640]{1,0:T(8,128)(2,1)S(1)} %bitcast.58), kind=kOutput, calls=%fused_computation.3 | convolution fusion | flops 419676160 | bytes 4259840 | tf_op jit(solution)/shard_map/dot_general | solution.py:587
  98.0 21.3 %route_6.1 = (bf16[128,2560]{1,0:T(8,128)(2,1)S(1)}, bf16[8,16,640]{2,1,0:T(8,128)(2,1)S(1)}) custom-call(s32[8]{0:T(128)S(1)} %select_reduce_fusion.1.block_for, f32[1,2560]{1,0:T(1,128)S(1)} %reshape.139.gain_ref, bf16[8,16,640]{2,1,0:T(8,128)(2,1)S(1)} %bitcast.56), custom_call_target="tpu_custom_call" | custom-call | tf_op jit(solution)/shard_map/route_6/pallas_call | solution.py:170
  119.3 0.4 fusion.18
  119.7 0.2 fusion.9
  119.9 0.1 copy.35
  120.1 0.7 subtract_convert_fusion.low_ref
  120.8 0.7 fusion.7.high_ref
  121.5 2.3 convolution_convert_fusion
  123.8 0.0 copy-done.2
  123.8 122.3 %experts.1.refs_0_ = bf16[4,128,640]{2,1,0:T(8,128)(2,1)} custom-call(bf16[8,64,2560]{2,1,0:T(8,128)(2,1)} %bitcast.63, bf16[2,2560,1536]{2,1,0:T(8,128)(2,1)} %gate_hbm.1, bf16[2,2560,1536]{2,1,0:T(8,128)(2,1)} %up_hbm.1, bf16[2,1536,2560]{2,1,0:T(8,128)(2,1)} %down_hbm.1, bf16[2560,768]{1,0:T(8,128)(2,1)} %shared_gate.1, bf16[2560,768]{1,0:T(8,128)(2,1)} %shared_up.1, ...), custom_call_target="tpu_custom_call" | custom-call | tf_op jit(solution)/shard_map/experts/pallas_call | solution.py:354
  246.2 10.2 %push_blk_11.1 = bf16[4,128,640]{2,1,0:T(8,128)(2,1)} custom-call(bf16[4,128,640]{2,1,0:T(8,128)(2,1)} %experts.1.refs_0_), custom_call_target="tpu_custom_call" | custom-call | tf_op jit(solution)/shard_map/push_blk_11/pallas_call | solution.py:75
  256.3 1.2 convert_reduce_fusion
  257.5 0.7 fusion.5
  (21 shorter events, 0.1 us)
Async XLA Ops:
  0.0 41.0 %copy-start = (bf16[2560,640]{1,0:T(8,128)(2,1)S(1)}, bf16[2560,640]{1,0:T(8,128)(2,1)}, u32[]{:S(2)}) copy-start(bf16[2560,640]{1,0:T(8,128)(2,1)} %param.21) | copy-start | bytes 9830404
  14.0 0.9 copy-start.9
  15.0 0.7 copy-start.12
  37.9 0.7 copy-start.7
  57.3 1.9 copy-start.3
  59.2 36.0 %copy-start.8 = (bf16[8,16,640]{2,1,0:T(8,128)(2,1)S(1)}, bf16[8,16,640]{2,1,0:T(8,128)(2,1)}, u32[]{:S(2)}) copy-start(bf16[8,16,640]{2,1,0:T(8,128)(2,1)} %copy-done.7) | copy-start | bytes 491524
  70.0 0.8 copy-start.4
  70.9 0.6 copy-start.11
  71.5 47.8 %copy-start.14 = (bf16[2560,64]{0,1:T(8,128)(2,1)S(1)}, bf16[2560,64]{0,1:T(8,128)(2,1)}, u32[]{:S(2)}) copy-start(bf16[2560,64]{0,1:T(8,128)(2,1)} %param.31) | copy-start | bytes 983044
  82.2 1.1 copy-start.5
  83.3 0.8 copy-start.10
  84.6 0.7 copy-start.6
  95.1 24.9 %copy-start.13 = (s32[128,512]{1,0:T(8,128)S(1)}, s32[128,512]{1,0:T(8,128)}, u32[]{:S(2)}) copy-start(s32[128,512]{1,0:T(8,128)} %copy.34) | copy-start | bytes 786436
  119.3 4.5 %copy-start.2 = (bf16[128,2560]{1,0:T(8,128)(2,1)}, bf16[128,2560]{1,0:T(8,128)(2,1)S(1)}, u32[]{:S(2)}) copy-start(bf16[128,2560]{1,0:T(8,128)(2,1)S(1)} %get-tuple-element.26.normed_ref) | copy-start | bytes 1966084
  123.8 134.5 %copy-start.1 = (bf16[2560,640]{1,0:T(8,128)(2,1)S(1)}, bf16[2560,640]{1,0:T(8,128)(2,1)}, u32[]{:S(2)}) copy-start(bf16[2560,640]{1,0:T(8,128)(2,1)} %param.21) | copy-start | bytes 9830404

commit v4 on v3

--- a/solution.py
+++ b/solution.py
@@ -458,8 +458,39 @@
     )(tail, q, kv, parent, cosines, sines, positions, cache)
 
 
-def merge_kernel(o_ref, lse_ref, out_ref):
-    n = o_ref.shape[0]
+def merge_kernel(n, part_ref, lse_part_ref, out_ref, o_ref, lse_ref, mine, send_sem, recv_sem, own_sem):
+    me = lax.axis_index("blk")
+    barrier = pltpu.get_barrier_semaphore()
+    partners = [lax.rem(me + k, n) for k in range(1, n)]
+    for to in partners:
+        pl.semaphore_signal(
+            barrier, inc=1, device_id={"blk": to}, device_id_type=pl.DeviceIdType.MESH
+        )
+    pl.semaphore_wait(barrier, n - 1)
+
+    def spread(phase, source, landing, whole):
+        copies = [
+            pltpu.make_async_remote_copy(
+                src_ref=source if whole else source.at[to],
+                dst_ref=landing.at[me],
+                send_sem=send_sem.at[phase, k],
+                recv_sem=recv_sem.at[phase, k],
+                device_id={"blk": to},
+                device_id_type=pl.DeviceIdType.MESH,
+            )
+            for k, to in enumerate(partners)
+        ]
+        copies.append(
+            pltpu.make_async_copy(
+                source if whole else source.at[me], landing.at[me], own_sem.at[phase]
+            )
+        )
+        for copy in copies:
+            copy.start()
+        return copies
+
+    for copy in spread(0, part_ref, o_ref, False) + spread(1, lse_part_ref, lse_ref, False):
+        copy.wait()
     peaks = lse_ref[0]
     for b in range(1, n):
         peaks = jnp.maximum(peaks, lse_ref[b])
@@ -473,19 +504,32 @@
         acc = o_ref[0, :, at].astype(jnp.float32) * scales[0][:, head : head + 1]
         for b in range(1, n):
             acc += o_ref[b, :, at].astype(jnp.float32) * scales[b][:, head : head + 1]
-        out_ref[:, at] = acc.astype(jnp.bfloat16)
-
-
-def merge(parts, lse):
+        mine[:, at] = acc.astype(jnp.bfloat16)
+    for copy in spread(2, mine, out_ref, True):
+        copy.wait()
+
+
+def merge(part, lse, collective_id):
+    n = part.shape[0]
     vmem = pl.BlockSpec(memory_space=pltpu.VMEM)
     return pl.pallas_call(
-        merge_kernel,
-        out_shape=jax.ShapeDtypeStruct(parts.shape[1:], jnp.bfloat16),
+        functools.partial(merge_kernel, n),
+        out_shape=jax.ShapeDtypeStruct(part.shape, jnp.bfloat16),
         in_specs=[vmem] * 2,
         out_specs=vmem,
-        compiler_params=pltpu.CompilerParams(vmem_limit_bytes=40 * MIB),
+        scratch_shapes=[
+            pltpu.VMEM(part.shape, part.dtype),
+            pltpu.VMEM(lse.shape, lse.dtype),
+            pltpu.VMEM(part.shape[1:], jnp.bfloat16),
+            pltpu.SemaphoreType.DMA((3, n)),
+            pltpu.SemaphoreType.DMA((3, n)),
+            pltpu.SemaphoreType.DMA((3,)),
+        ],
+        compiler_params=pltpu.CompilerParams(
+            collective_id=collective_id, has_side_effects=True, vmem_limit_bytes=40 * MIB
+        ),
         name="merge",
-    )(parts, lse)
+    )(part, lse)
 
 
 def inverse_of(migration):
@@ -576,11 +620,7 @@
         prompt_cache.reshape(pages_local * page_length, features),
     )
     share = rows // n_blk
-    parts, lses = push(
-        [part.reshape(n_blk, share, -1), lse.reshape(n_blk, share, HEAD_WIDTH)], "blk", 4
-    )
-    heads_mine = merge(parts, lses)
-    (heads,) = push([heads_mine], "blk", 5, gather=True)
+    heads = merge(part.reshape(n_blk, share, -1), lse.reshape(n_blk, share, HEAD_WIDTH), 4)
     heads = heads.reshape(rows, -1)
     attended_there = (
         x_local.astype(jnp.float32)

time: 259 us -> 251 us (0.969)
  local copies, waits for them, and re-layouts: 19.4 us -> 15.4 us
    pallas_call x4 -> x2, Pallas kernels: 43.4 us -> 22.9 us  [push(): pl.pallas_call(functools.partial(push_kernel, axis, n, count, gather), ou...]
    pallas_call x1, Pallas kernels: 0.46 us -> 19.2 us  [merge(): pl.pallas_call(functools.partial(merge_kernel, n), out_shape=jax.ShapeDty...]
    unnamed x31 -> x23, local copies, waits for them, and re-layouts: 8.18 us -> 4.15 us
where the time goes in v4:
time: 251 us
  Pallas kernels  219 us (87%)
  local copies, waits for them, and re-layouts  15.4 us (6%)
  matrix products  7.36 us (3%)
  other arithmetic  6.46 us (3%)
    pallas_call x1, Pallas kernels, run_experts(): pl.pallas_call(functools.partial(experts_kernel, n), out_shape=jax.ShapeD...  122 us
    pallas_call x2, Pallas kernels, route_rows(): pl.pallas_call(functools.partial(route_kernel, n, n_blk, extra), out_shap...  44.6 us
    pallas_call x2, Pallas kernels, push(): pl.pallas_call(functools.partial(push_kernel, axis, n, count, gather), ou...  22.9 us
    pallas_call x1, Pallas kernels, merge(): pl.pallas_call(functools.partial(merge_kernel, n), out_shape=jax.ShapeDty...  19.2 us
    pallas_call x1, Pallas kernels, attention_part(): pl.pallas_call(attention_kernel, out_shape=[jax.ShapeDtypeStruct(q.shape,...  10.9 us

profile of v4, /device:TPU:9, one launch (start us, length us, event | category | flops | bytes accessed | tf_op | source)
XLA Modules:
  0.0 250.7 jit_solution(4675116197055151731)
XLA Ops:
  0.0 0.0 copy-start
  0.0 1.4 dynamic_slice.15
  3.3 1.2 dynamic_slice.14
  4.6 0.7 pad_add_fusion.tail_ref
  5.3 0.7 dynamic-slice_bitcast_fusion
  6.0 0.1 select_reduce_fusion
  6.1 0.7 fusion.17
  6.7 0.7 pad.5.refs_0_
  7.4 0.8 select_reduce_fusion.1.block_for
  8.2 0.1 iota_add_fusion
  8.3 0.1 add.131
  8.3 0.8 eq.132
  9.1 0.1 compare_reduce_fusion
  9.2 0.1 fusion.4
  9.4 0.1 add_bitcast_fusion
  9.5 0.1 eq.140
  9.5 0.7 reshape.140.gain_ref
  10.3 0.7 reshape.139.gain_ref
  11.0 0.1 bitcast_compare_fusion
  11.1 0.3 fusion.11
  11.4 0.1 pad_maximum_fusion
  11.5 0.7 eq.143
  12.3 1.8 copy.34
  14.0 0.0 copy-start.6
  14.0 0.9 copy-done.6
  15.0 0.0 copy-start.7
  15.0 0.7 copy-done.7
  15.6 22.3 %route_0.1 = (bf16[128,2560]{1,0:T(8,128)(2,1)S(1)}, bf16[8,16,640]{2,1,0:T(8,128)(2,1)S(1)}, s32[8,1,128]{2,1,0:T(1,128)S(1)}) custom-call(s32[8]{0:T(128)S(1)} %copy-done.7, f32[1,2560]{1,0:T(1,128)S(1)} %reshape.140.gain_ref, bf16[8,16,640]{2,1,0:T(8,128)(2,1)S(1)} %bitcast.61, s32[1,128]{1,0:T(1,128)S(1)} %pad.5.refs_0_), custom_call_target="tpu_custom_call" | custom-call | tf_op jit(solution)/shard_map/route_0/pallas_call | solution.py:170
  37.9 0.0 copy-start.4
  37.9 0.7 copy-done.4
  38.6 0.1 concatenate.9
  38.7 0.1 fusion.8.parent_ref
  38.8 2.3 convolution_convert_fusion.2.refs_1_
  41.1 0.0 copy-done
  41.1 1.3 convolution_convert_fusion.1.refs_0_
  42.4 12.8 %push_blk_3.1 = (bf16[4,128,640]{2,1,0:T(8,128)(2,1)}, bf16[4,128,256]{2,1,0:T(8,128)(2,1)}) custom-call(bf16[128,640]{1,0:T(8,128)(2,1)} %convolution_convert_fusion.1.refs_0_, bf16[128,256]{1,0:T(8,128)(2,1)} %convolution_convert_fusion.2.refs_1_), custom_call_target="tpu_custom_call" | custom-call | tf_op jit(solution)/shard_map/push_blk_3/pallas_call | solution.py:75
  55.2 1.1 copy.36
  56.3 0.0 copy-start.5
  56.3 1.0 copy.37
  57.3 0.0 copy-start.3
  57.4 1.9 copy-done.3
  59.2 10.9 %attention_part.1 = (bf16[128,2560]{1,0:T(8,128)(2,1)S(1)}, f32[128,128]{1,0:T(8,128)S(1)}) custom-call(s32[2]{0:T(128)S(1)} %pad_add_fusion.tail_ref, bf16[128,2560]{1,0:T(8,128)(2,1)S(1)} %bitcast.54, bf16[128,1024]{1,0:T(8,128)(2,1)S(1)} %bitcast.56, bf16[128,128]{1,0:T(8,128)(2,1)S(1)} %fusion.8.parent_ref, f32[128,128]{1,0:T(8,128)S(1)} %get-tuple-element.28.cos_ref, ...), custom_call_target="tpu_custom_call" | custom-call | tf_op jit(solution)/shard_map/attention_part/pallas_call | solution.py:448
  70.1 0.0 copy-start.10
  70.1 19.2 %merge.1 = bf16[4,32,2560]{2,1,0:T(8,128)(2,1)S(1)} custom-call(bf16[4,32,2560]{2,1,0:T(8,128)(2,1)S(1)} %bitcast.58, f32[4,32,128]{2,1,0:T(8,128)S(1)} %bitcast.62), custom_call_target="tpu_custom_call" | custom-call | tf_op jit(solution)/shard_map/merge/pallas_call | solution.py:515
  89.3 0.0 copy-start.9
  89.3 0.0 copy-done.5
  89.4 0.0 copy-done.8
  89.4 0.7 fusion
  90.1 22.3 %route_6.1 = (bf16[128,2560]{1,0:T(8,128)(2,1)S(1)}, bf16[8,16,640]{2,1,0:T(8,128)(2,1)S(1)}) custom-call(s32[8]{0:T(128)S(1)} %select_reduce_fusion.1.block_for, f32[1,2560]{1,0:T(1,128)S(1)} %reshape.139.gain_ref, bf16[8,16,640]{2,1,0:T(8,128)(2,1)S(1)} %bitcast.57), custom_call_target="tpu_custom_call" | custom-call | tf_op jit(solution)/shard_map/route_6/pallas_call | solution.py:170
  112.3 0.0 copy-start.2
  112.3 0.0 copy-done.10
  112.4 0.4 fusion.18
  112.7 0.2 fusion.9
  112.9 0.1 copy.35
  113.1 0.0 copy-done.9
  113.1 0.7 subtract_convert_fusion.low_ref
  113.8 0.7 fusion.7.high_ref
  114.5 2.3 convolution_convert_fusion
  116.8 0.0 copy-done.2
  116.8 121.8 %experts.1.refs_0_ = bf16[4,128,640]{2,1,0:T(8,128)(2,1)} custom-call(bf16[8,64,2560]{2,1,0:T(8,128)(2,1)} %bitcast.64, bf16[2,2560,1536]{2,1,0:T(8,128)(2,1)} %gate_hbm.1, bf16[2,2560,1536]{2,1,0:T(8,128)(2,1)} %up_hbm.1, bf16[2,1536,2560]{2,1,0:T(8,128)(2,1)} %down_hbm.1, bf16[2560,768]{1,0:T(8,128)(2,1)} %shared_gate.1, bf16[2560,768]{1,0:T(8,128)(2,1)} %shared_up.1, ...), custom_call_target="tpu_custom_call" | custom-call | tf_op jit(solution)/shard_map/experts/pallas_call | solution.py:354
  238.6 10.2 %push_blk_11.1 = bf16[4,128,640]{2,1,0:T(8,128)(2,1)} custom-call(bf16[4,128,640]{2,1,0:T(8,128)(2,1)} %experts.1.refs_0_), custom_call_target="tpu_custom_call" | custom-call | tf_op jit(solution)/shard_map/push_blk_11/pallas_call | solution.py:75
  248.8 1.2 convert_reduce_fusion
  250.0 0.7 fusion.5
  250.7 0.0 copy-done.1
  (11 shorter events, 0.1 us)
Async XLA Ops:
  0.0 41.1 %copy-start = (bf16[2560,640]{1,0:T(8,128)(2,1)S(1)}, bf16[2560,640]{1,0:T(8,128)(2,1)}, u32[]{:S(2)}) copy-start(bf16[2560,640]{1,0:T(8,128)(2,1)} %param.21) | copy-start | bytes 9830404
  14.0 0.9 copy-start.6
  15.0 0.7 copy-start.7
  37.9 0.7 copy-start.4
  56.3 33.0 %copy-start.5 = (bf16[8,16,640]{2,1,0:T(8,128)(2,1)S(1)}, bf16[8,16,640]{2,1,0:T(8,128)(2,1)}, u32[]{:S(2)}) copy-start(bf16[8,16,640]{2,1,0:T(8,128)(2,1)} %copy-done.4) | copy-start | bytes 491524
  57.3 1.9 copy-start.3
  59.2 30.1 %copy-start.8 = (bf16[2560,640]{1,0:T(8,128)(2,1)S(1)}, bf16[2560,640]{1,0:T(8,128)(2,1)}, u32[]{:S(2)}) copy-start(bf16[2560,640]{1,0:T(8,128)(2,1)} %param.23) | copy-start | bytes 9830404
  70.1 42.2 %copy-start.10 = (bf16[2560,64]{0,1:T(8,128)(2,1)S(1)}, bf16[2560,64]{0,1:T(8,128)(2,1)}, u32[]{:S(2)}) copy-start(bf16[2560,64]{0,1:T(8,128)(2,1)} %param.31) | copy-start | bytes 983044
  89.3 23.8 %copy-start.9 = (s32[128,512]{1,0:T(8,128)S(1)}, s32[128,512]{1,0:T(8,128)}, u32[]{:S(2)}) copy-start(s32[128,512]{1,0:T(8,128)} %copy.34) | copy-start | bytes 786436
  112.3 4.5 %copy-start.2 = (bf16[128,2560]{1,0:T(8,128)(2,1)}, bf16[128,2560]{1,0:T(8,128)(2,1)S(1)}, u32[]{:S(2)}) copy-start(bf16[128,2560]{1,0:T(8,128)(2,1)S(1)} %get-tuple-element.22.normed_ref) | copy-start | bytes 1966084
  116.8 133.9 %copy-start.1 = (bf16[2560,640]{1,0:T(8,128)(2,1)S(1)}, bf16[2560,640]{1,0:T(8,128)(2,1)}, u32[]{:S(2)}) copy-start(bf16[2560,640]{1,0:T(8,128)(2,1)} %param.21) | copy-start | bytes 9830404
